TPU v7x, 512 devices: a whole 4x8x8 slice. The times are simulated.
512 devices in a mesh: replica: 16 (over z_lo, y), fsdp: 32 (over x, z_hi, core).
Axes of the slice: x: 4, y: 8, z: 8 (z_hi: 4, z_lo: 2; z = z_hi * 2 + z_lo), core: 2. Of those that a mesh axis runs over, the one named last changes fastest.
Arguments:
- activations: bfloat16 [131072, 4096], P(('replica', 'fsdp')), may hold values from -6 to 6
- cotangent: bfloat16 [131072, 512], P(('replica', 'fsdp')), may hold values from -6 to 6
- local_weight: float32 [16, 4096, 512], P('replica', 'fsdp'), may hold values from -6 to 6
- first_moment: float32 [16, 4096, 512], P('replica', 'fsdp'), may hold values from -4 to 4
- second_moment: float32 [16, 4096, 512], P('replica', 'fsdp'), may hold values from 0.25 to 4
- anchor_weight: float32 [4096, 512], P('fsdp'), may hold values from -6 to 6
- outer_momentum: float32 [4096, 512], P('fsdp'), may hold values from -3 to 3
Outputs:
- key_out: bfloat16 [131072, 512], P(('replica', 'fsdp'))
- new_weight: float32 [16, 4096, 512], P('replica', 'fsdp')
- new_first: float32 [16, 4096, 512], P('replica', 'fsdp')
- new_second: float32 [16, 4096, 512], P('replica', 'fsdp')
- new_anchor: float32 [4096, 512], P('fsdp')
- new_momentum: float32 [4096, 512], P('fsdp')
All inputs are finite; a program needn't handle non-finite values.
Results may differ from a plain program's by a relative error of at most 0.012.
Values may be sent and summed in bfloat16 or wider, within the bound.
No kernel may reach another device: no remote copies, remote signals or barrier semaphores. Data moves between devices by JAX's collectives and lax.ppermute only.
A program may use at most 64 MiB of HBM per device.

v0:
```python
import jax
import jax.numpy as jnp
from jax import lax
from jax.sharding import PartitionSpec as P


def outer_update(summed, anchor_part, momentum_part, replicas):
    pseudo = anchor_part - summed * (1.0 / replicas)
    momentum_next = 0.9 * momentum_part + pseudo
    anchor_next = anchor_part - 0.7 * (pseudo + 0.9 * momentum_next)
    return (anchor_next, momentum_next)


def shards(
    activations, cotangent, local_weight, first_moment, second_moment, anchor_weight, outer_momentum
):
    scale_factor = activations.shape[1] ** (-0.5)
    weight = local_weight[0]
    weight_half = weight.astype(jnp.bfloat16)
    columns = activations
    keys = jnp.dot(
        columns,
        lax.all_gather(weight_half, "fsdp", axis=0, tiled=True),
        preferred_element_type=jnp.float32,
    )
    key_out = (keys * scale_factor).astype(jnp.bfloat16)
    columns = activations
    grad_sum = lax.psum_scatter(
        lax.dot_general(
            columns, cotangent, (((0,), (0,)), ((), ())), preferred_element_type=jnp.float32
        ).astype(jnp.bfloat16),
        "fsdp",
        scatter_dimension=0,
        tiled=True,
    ).astype(jnp.float32)
    grad = grad_sum * scale_factor
    new_first = 0.9 * first_moment[0] + 0.1 * grad
    new_second = 0.95 * second_moment[0] + 0.05 * grad * grad
    stepped = weight - 0.02 * (new_first / (jnp.sqrt(new_second) + 1e-08) + 0.1 * weight)
    replicas = lax.axis_size("replica")
    summed = lax.psum(weight.astype(jnp.bfloat16), "replica").astype(jnp.float32)
    new_anchor, new_momentum = outer_update(summed, anchor_weight, outer_momentum, replicas)
    new_weight = 0.5 * stepped + 0.5 * new_anchor
    return (key_out, new_weight[None], new_first[None], new_second[None], new_anchor, new_momentum)


def solution(mesh):
    return jax.shard_map(
        shards,
        mesh=mesh,
        in_specs=(
            P(("replica", "fsdp"), None),
            P(("replica", "fsdp"), None),
            P("replica", "fsdp", None),
            P("replica", "fsdp", None),
            P("replica", "fsdp", None),
            P("fsdp", None),
            P("fsdp", None),
        ),
        out_specs=(
            P(("replica", "fsdp"), None),
            P("replica", "fsdp", None),
            P("replica", "fsdp", None),
            P("replica", "fsdp", None),
            P("fsdp", None),
            P("fsdp", None),
        ),
        check_vma=False,
    )
```

profile of v0, /device:TPU:2, one launch (start us, length us, event | category | flops | bytes accessed | tf_op | source)
XLA Modules:
  0.0 342.2 jit_solution(9101880632263601950)
XLA Ops:
  7.2 0.0 copy-start
  7.2 0.0 all-gather.2.cloned.1.call-start
  7.2 1.8 bitcast_convert_fusion
  9.0 0.0 all-gather.2.cloned.1.call-update
  9.0 0.0 reduce-scatter.2.cloned.1.call-start
  9.1 0.0 copy-done
  9.1 4.2 %convolution_convert_fusion = bf16[4096,512]{1,0:T(8,128)(2,1)} fusion(bf16[256,4096]{1,0:T(8,128)(2,1)S(1)} %copy-done, bf16[256,512]{1,0:T(8,128)(2,1)} %param.8), kind=kOutput, calls=%fused_computation | convolution fusion | flops 1075838976 | bytes 6553600 | tf_op jit(solution)/shard_map/dot_general | solution.py:29
  13.3 0.0 reduce-scatter.2.cloned.1.call-update
  13.3 0.0 copy-start.1
  13.3 0.0 copy-start.2
  13.3 0.0 copy-start.3
  13.3 0.0 copy-start.4
  13.4 0.0 copy-start.5
  13.4 68.4 %all-gather.2.cloned.1.call-done = bf16[4096,512]{1,0:T(8,128)(2,1)} async-done(((bf16[128,512]{1,0:T(8,128)(2,1)}), bf16[4096,512]{1,0:T(8,128)(2,1)}) %all-gather.2.cloned.1.call-update) | async-done | bytes 4194320 | tf_op jit(solution)/shard_map/all_gather | solution.py:23
  81.8 0.0 all-reduce.2.cloned.1.call-start
  81.8 0.7 all-reduce.2.cloned.1.call-update
  82.5 4.1 %fusion = bf16[256,512]{1,0:T(8,128)(2,1)} fusion(bf16[256,4096]{1,0:T(8,128)(2,1)S(1)} %copy-done, bf16[4096,512]{1,0:T(8,128)(2,1)} %all-gather.2.cloned.1.call-done), kind=kOutput, calls=%fused_computation.2 | convolution fusion | flops 1074003968 | bytes 6553600 | tf_op jit(solution)/shard_map/dot_general | solution.py:21
  86.6 106.5 %reduce-scatter.2.cloned.1.call-done = bf16[128,512]{1,0:T(8,128)(2,1)} async-done(((bf16[4096,512]{1,0:T(8,128)(2,1)}), bf16[128,512]{1,0:T(8,128)(2,1)}) %reduce-scatter.2.cloned.1.call-update) | async-done | bytes 131088 | tf_op jit(solution)/shard_map/reduce_scatter | solution.py:28
  193.1 140.5 %all-reduce.2.cloned.1.call-done = bf16[128,512]{1,0:T(8,128)(2,1)} async-done(((bf16[128,512]{1,0:T(8,128)(2,1)}), bf16[128,512]{1,0:T(8,128)(2,1)}) %all-reduce.2.cloned.1.call-update) | async-done | bytes 131088 | tf_op jit(solution)/shard_map/psum | solution.py:41
  333.6 0.0 copy-done.1
  333.6 0.0 copy-done.2
  333.6 0.0 copy-done.3
  333.6 0.0 copy-done.4
  333.6 0.0 copy-done.5
  333.6 2.1 fusion.8
Async XLA Ops:
  7.2 1.9 copy-start
  7.2 74.6 %all-gather.2.cloned.1.call-start = ((), (), s32[]{:S(2)}) async-start(), calls=%async_computation.1 | async-start | bytes 4325376 | tf_op jit(solution)/shard_map/all_gather | solution.py:23
  9.0 184.1 %reduce-scatter.2.cloned.1.call-start = ((), (), s32[]{:S(2)}) async-start(), calls=%async_computation.2 | async-start | bytes 4325376 | tf_op jit(solution)/shard_map/reduce_scatter | solution.py:28
  13.3 320.3 %copy-start.1 = (f32[1,128,512]{2,1,0:T(8,128)S(1)}, f32[1,128,512]{2,1,0:T(8,128)}, u32[]{:S(2)}) copy-start(f32[1,128,512]{2,1,0:T(8,128)} %param.9) | copy-start | bytes 786436
  13.3 320.3 %copy-start.2 = (f32[1,128,512]{2,1,0:T(8,128)S(1)}, f32[1,128,512]{2,1,0:T(8,128)}, u32[]{:S(2)}) copy-start(f32[1,128,512]{2,1,0:T(8,128)} %param.10) | copy-start | bytes 786436
  13.3 320.2 %copy-start.3 = (f32[1,128,512]{2,1,0:T(8,128)S(1)}, f32[1,128,512]{2,1,0:T(8,128)}, u32[]{:S(2)}) copy-start(f32[1,128,512]{2,1,0:T(8,128)} %param.11) | copy-start | bytes 786436
  13.3 320.2 %copy-start.4 = (f32[128,512]{1,0:T(8,128)S(1)}, f32[128,512]{1,0:T(8,128)}, u32[]{:S(2)}) copy-start(f32[128,512]{1,0:T(8,128)} %param.12) | copy-start | bytes 786436
  13.4 320.2 %copy-start.5 = (f32[128,512]{1,0:T(8,128)S(1)}, f32[128,512]{1,0:T(8,128)}, u32[]{:S(2)}) copy-start(f32[128,512]{1,0:T(8,128)} %param.13) | copy-start | bytes 786436
  81.8 251.8 %all-reduce.2.cloned.1.call-start = ((), (), s32[]{:S(2)}) async-start(), calls=%async_computation.3 | async-start | bytes 262144 | tf_op jit(solution)/shard_map/psum | solution.py:41
Sparse Core Ops, SparseCore 0:
  11.7 70.0 all-gather.1
  86.3 106.7 reduce-scatter.1
  196.9 136.6 all-reduce.1
where the time goes:
time: 342 us
  waiting for transfers between devices  316 us (92%)
  between operations  13.8 us (4%)
  matrix products  8.35 us (2%)
  other arithmetic  3.88 us (1%)
    psum x1, waiting for transfers between devices, shards(): lax.psum(weight.astype(jnp.bfloat16), 'replica').astype(jnp.float32)  140 us
    reduce_scatter x1, waiting for transfers between devices, shards(): lax.psum_scatter(lax.dot_general(columns, cotangent, (((0,), (0,)), ((),...  106 us
    all_gather x1, waiting for transfers between devices, shards(): lax.all_gather(weight_half, 'fsdp', axis=0, tiled=True)  68.4 us
  transfers between devices with their start and end apart: 3, of which 3 were waited for; matrix products, arithmetic and copies ran while one was open for 2% of the time, Pallas kernels for 0%

commit v1 on v0

v1 whole, which is shorter than its diff:
```python
import jax
import jax.numpy as jnp
from jax import lax
from jax.sharding import Mesh, PartitionSpec as P

REPLICA = ("zl", "y")
FSDP = ("x", "zh", "core")
F32 = jnp.float32
BF16 = jnp.bfloat16


def outer_update(summed, anchor_part, momentum_part, replicas):
    pseudo = anchor_part - summed * (1.0 / replicas)
    momentum_next = 0.9 * momentum_part + pseudo
    anchor_next = anchor_part - 0.7 * (pseudo + 0.9 * momentum_next)
    return (anchor_next, momentum_next)


def exchange(blocks, axis):
    return lax.all_to_all(blocks, axis, 0, 0, tiled=True)


def gather(block, axis):
    count = lax.axis_size(axis)
    return exchange(jnp.broadcast_to(block[None], (count,) + block.shape), axis)


def total(blocks):
    return jnp.sum(blocks.astype(F32), axis=0)


def swap(block):
    return lax.ppermute(block, "core", [(0, 1), (1, 0)])


def columns_of(x, parity):
    tokens, width = x.shape
    pairs = [
        lax.select(
            parity == 0, x[:, at : at + 128], x[:, at + 128 : at + 256]
        )
        for at in range(0, width, 256)
    ]
    return jnp.concatenate(pairs, axis=1)


def shards(
    activations, cotangent, local_weight, first_moment, second_moment, anchor_weight, outer_momentum
):
    tokens, width = activations.shape
    rows, features = anchor_weight.shape
    scale_factor = width ** (-0.5)
    core = lax.axis_index("core")
    weight = local_weight[0]
    weight_half = weight.astype(BF16)

    theirs = swap(columns_of(activations, 1 - core))
    their_cotangent = swap(cotangent)
    mine = columns_of(activations, core)

    column = gather(weight_half, "zh").reshape(-1, features)
    half = gather(column, "x").reshape(-1, features)

    term = lax.dot_general(
        jnp.concatenate([mine, theirs], axis=0),
        jnp.concatenate([cotangent, their_cotangent], axis=0),
        (((0,), (0,)), ((), ())),
        preferred_element_type=F32,
    ).astype(BF16)
    part = total(exchange(term.reshape(4, -1, features), "x")).astype(BF16)
    grad_sum = total(exchange(part.reshape(4, rows, features), "zh"))
    grad = grad_sum * scale_factor

    replicas = lax.axis_size(REPLICA)
    pieces = exchange(weight_half.reshape(replicas, -1, features), REPLICA)
    summed = gather(total(pieces).astype(BF16), REPLICA).reshape(rows, features).astype(F32)

    their_keys = swap(jnp.dot(theirs, half, preferred_element_type=F32))
    keys = jnp.dot(mine, half, preferred_element_type=F32) + their_keys
    key_out = (keys * scale_factor).astype(BF16)

    new_first = 0.9 * first_moment[0] + 0.1 * grad
    new_second = 0.95 * second_moment[0] + 0.05 * grad * grad
    stepped = weight - 0.02 * (new_first / (jnp.sqrt(new_second) + 1e-08) + 0.1 * weight)
    new_anchor, new_momentum = outer_update(summed, anchor_weight, outer_momentum, replicas)
    new_weight = 0.5 * stepped + 0.5 * new_anchor
    return (key_out, new_weight[None], new_first[None], new_second[None], new_anchor, new_momentum)


def solution(mesh):
    fine = Mesh(mesh.devices.reshape(2, 8, 4, 4, 2), REPLICA + FSDP)
    return jax.shard_map(
        shards,
        mesh=fine,
        in_specs=(
            P(REPLICA + FSDP, None),
            P(REPLICA + FSDP, None),
            P(REPLICA, FSDP, None),
            P(REPLICA, FSDP, None),
            P(REPLICA, FSDP, None),
            P(FSDP, None),
            P(FSDP, None),
        ),
        out_specs=(
            P(REPLICA + FSDP, None),
            P(REPLICA, FSDP, None),
            P(REPLICA, FSDP, None),
            P(REPLICA, FSDP, None),
            P(FSDP, None),
            P(FSDP, None),
        ),
        check_vma=False,
    )
```

time: 342 us -> 156 us (0.46)
  the two profiles are of different devices: /device:TPU:2 before, /device:TPU:8 now
where the time goes in v1:
time: 156 us; the launch traced here: 155 us
  blocking collectives  43.2 us (28%)
  starting transfers between devices  39 us (25%)
  waiting for transfers between devices  37.2 us (24%)
  other arithmetic  21.5 us (14%)
  matrix products  9.16 us (6%)
  local copies, waits for them, and re-layouts  4.01 us (3%)
    all_to_all x2, blocking collectives, exchange(): return lax.all_to_all(blocks, axis, 0, 0, tiled=True)  43.2 us
    all_to_all x4, waiting for transfers between devices, exchange(): return lax.all_to_all(blocks, axis, 0, 0, tiled=True)  36.4 us
    all_to_all x4, starting transfers between devices, exchange(): return lax.all_to_all(blocks, axis, 0, 0, tiled=True)  33.2 us
    unnamed x15, other arithmetic  16 us
    ppermute x3, starting transfers between devices, swap(): return lax.ppermute(block, 'core', [(0, 1), (1, 0)])  5.74 us
    dot_general x1, matrix products, shards(): lax.dot_general(jnp.concatenate([mine, theirs], axis=0), jnp.concatenate(...  4.18 us
  transfers between devices with their start and end apart: 7, of which 5 were waited for; matrix products, arithmetic and copies ran while one was open for 9% of the time, Pallas kernels for 0%

profile of v1, /device:TPU:8, one launch (start us, length us, event | category | flops | bytes accessed | tf_op | source)
XLA Modules:
  0.0 154.8 jit_solution(13683208240780302453)
XLA Ops:
  0.6 0.0 copy-start
  0.7 1.7 %constant_dynamic-update-slice_fusion.31 = bf16[256,2048]{1,0:T(8,128)(2,1)} fusion(pred[]{:T(512)S(6)} %eq.5, bf16[256,4096]{1,0:T(8,128)(2,1)} %param.7), kind=kLoop, calls=%fused_computation.57 | loop fusion | flops 32767 | bytes 196609
  2.3 1.6 %constant_dynamic-update-slice_fusion.30 = (bf16[256,2048]{1,0:T(8,128)(2,1)}, bf16[256,2048]{1,0:T(8,128)(2,1)S(1)}) fusion(bf16[256,2048]{1,0:T(8,128)(2,1)} %constant_dynamic-update-slice_fusion.31, pred[]{:T(512)S(6)} %eq.5, bf16[256,4096]{1,0:T(8,128)(2,1)} %param.7, pred[]{:T(512)S(6)} %eq.4), kind=kLoop, calls=%fused_computation.56 | loop fusion | flops 65535 | bytes 393218
  3.9 1.6 %constant_dynamic-update-slice_fusion.29 = (bf16[256,2048]{1,0:T(8,128)(2,1)}, bf16[256,2048]{1,0:T(8,128)(2,1)S(1)}) fusion(bf16[256,2048]{1,0:T(8,128)(2,1)} %get-tuple-element.37, pred[]{:T(512)S(6)} %eq.5, bf16[256,4096]{1,0:T(8,128)(2,1)} %param.7, bf16[256,2048]{1,0:T(8,128)(2,1)S(1)} %get-tuple-element.38, pred[]{:T(512)S(6)} %eq.4), kind=kLoop, calls=%fused_computation.55 | loop fusion | flops 65536 | bytes 393218
  5.5 1.6 %constant_dynamic-update-slice_fusion.28 = (bf16[256,2048]{1,0:T(8,128)(2,1)}, bf16[256,2048]{1,0:T(8,128)(2,1)S(1)}) fusion(bf16[256,2048]{1,0:T(8,128)(2,1)} %get-tuple-element.35, pred[]{:T(512)S(6)} %eq.5, bf16[256,4096]{1,0:T(8,128)(2,1)} %param.7, bf16[256,2048]{1,0:T(8,128)(2,1)S(1)} %get-tuple-element.36, pred[]{:T(512)S(6)} %eq.4), kind=kLoop, calls=%fused_computation.54 | loop fusion | flops 65536 | bytes 393218
  7.2 1.6 %constant_dynamic-update-slice_fusion.27 = (bf16[256,2048]{1,0:T(8,128)(2,1)}, bf16[256,2048]{1,0:T(8,128)(2,1)S(1)}) fusion(bf16[256,2048]{1,0:T(8,128)(2,1)} %get-tuple-element.33, pred[]{:T(512)S(6)} %eq.5, bf16[256,4096]{1,0:T(8,128)(2,1)} %param.7, bf16[256,2048]{1,0:T(8,128)(2,1)S(1)} %get-tuple-element.34, pred[]{:T(512)S(6)} %eq.4), kind=kLoop, calls=%fused_computation.53 | loop fusion | flops 65536 | bytes 393218
  8.8 0.0 copy-start.3
  8.8 1.7 %constant_dynamic-update-slice_fusion.26 = (bf16[256,2048]{1,0:T(8,128)(2,1)}, bf16[256,2048]{1,0:T(8,128)(2,1)S(1)}) fusion(bf16[256,2048]{1,0:T(8,128)(2,1)} %get-tuple-element.31, pred[]{:T(512)S(6)} %eq.5, bf16[256,4096]{1,0:T(8,128)(2,1)} %param.7, bf16[256,2048]{1,0:T(8,128)(2,1)S(1)} %get-tuple-element.32, pred[]{:T(512)S(6)} %eq.4), kind=kLoop, calls=%fused_computation.52 | loop fusion | flops 65536 | bytes 393218
  10.5 0.0 copy-done
  10.5 0.7 constant_dynamic-update-slice_fusion.25
  11.2 0.7 constant_dynamic-update-slice_fusion.24
  11.8 0.7 constant_dynamic-update-slice_fusion.23
  12.5 0.7 constant_dynamic-update-slice_fusion.22
  13.2 0.7 constant_dynamic-update-slice_fusion.21
  13.9 0.7 constant_dynamic-update-slice_fusion.20
  14.6 0.0 copy-start.8
  14.6 0.7 constant_dynamic-update-slice_fusion.19
  15.3 0.7 constant_dynamic-update-slice_fusion.18
  16.0 0.7 constant_dynamic-update-slice_fusion.17
  16.7 0.7 constant_dynamic-update-slice_fusion.16
  17.4 0.0 copy-start.6
  17.4 1.0 copy-done.6
  18.3 1.9 %collective-permute-start = (bf16[256,2048]{1,0:T(8,128)(2,1)}, bf16[256,2048]{1,0:T(8,128)(2,1)}, u32[]{:S(2)}, u32[]{:S(2)}) collective-permute-start(bf16[256,2048]{1,0:T(8,128)(2,1)} %get-tuple-element.9), channel_id=1, source_target_pairs={{0,1},{1,0},{2,3},{3,2},{4,5},{5,4},{6,7},{7,6},{8,9},{9,8},{10,11... | collective-permute-start | bytes 3145736 | tf_op jit(solution)/shard_map/ppermute | solution.py:33
  20.3 0.0 copy-done.3
  20.3 17.7 %all_to_all.30 = bf16[16,8,512]{2,1,0:T(8,128)(2,1)S(1)} all-to-all(bf16[16,8,512]{2,1,0:T(8,128)(2,1)S(1)} %get-tuple-element.41), channel_id=1, replica_groups=mesh['zl'=2,'y'=8,'x'=4,'zh'=4,'core'=2] {'zl','y'}, dimensions={0} | all-to-all | bytes 262144 | tf_op jit(solution)/shard_map/all_to_all | solution.py:20
  38.0 0.9 broadcast_in_dim.13
  38.8 9.4 %all-to-all-start = ((bf16[4,128,512]{2,1,0:T(8,128)(2,1)}), bf16[4,128,512]{2,1,0:T(8,128)(2,1)S(1)}, u32[]{:S(2)}, u32[]{:S(2)}) async-start(bf16[4,128,512]{2,1,0:T(8,128)(2,1)} %broadcast_in_dim.13), calls=%async_computation | async-start | bytes 1048576 | tf_op jit(solution)/shard_map/all_to_all | solution.py:20
  48.2 0.0 copy-done.8
  48.2 1.9 %collective-permute-start.2 = (bf16[256,512]{1,0:T(8,128)(2,1)S(1)}, bf16[256,512]{1,0:T(8,128)(2,1)S(1)}, u32[]{:S(2)}, u32[]{:S(2)}) collective-permute-start(bf16[256,512]{1,0:T(8,128)(2,1)S(1)} %copy-done.8), channel_id=1, source_target_pairs={{0,1},{1,0},{2,3},{3,2},{4,5},{5,4},{6,7},{7,6},{8,9},{9,8},{10,11... | collective-permute-start | bytes 786440 | tf_op jit(solution)/shard_map/ppermute | solution.py:33
  50.1 0.7 constant_dynamic-update-slice_fusion
  50.8 0.8 collective-permute-done.2
  51.6 0.0 collective-permute-done
  51.6 4.2 %convolution_convert_fusion = bf16[2048,512]{1,0:T(8,128)(2,1)} fusion(bf16[256,2048]{1,0:T(8,128)(2,1)} %collective-permute-done, bf16[256,2048]{1,0:T(8,128)(2,1)} %constant_dynamic-update-slice_fusion, bf16[256,512]{1,0:T(8,128)(2,1)S(1)} %collective-permute-done.2, bf16[256,512]{1,0:T(8,128)(2,1)S(1)} %copy-done.8), kind=kOutput, calls=%fused_computation | convolution fusion | flops 1080033280 | bytes 4718592 | tf_op jit(solution)/shard_map/dot_general | solution.py:64
  55.8 6.9 %all-to-all-done = bf16[4,128,512]{2,1,0:T(8,128)(2,1)S(1)} async-done(((bf16[4,128,512]{2,1,0:T(8,128)(2,1)}), bf16[4,128,512]{2,1,0:T(8,128)(2,1)S(1)}, u32[]{:S(2)}, u32[]{:S(2)}) %all-to-all-start) | async-done | bytes 524320 | tf_op jit(solution)/shard_map/all_to_all | solution.py:20
  62.7 25.6 %all_to_all.31 = bf16[4,512,512]{2,1,0:T(8,128)(2,1)S(1)} all-to-all(bf16[4,512,512]{2,1,0:T(8,128)(2,1)} %bitcast.58), channel_id=1, replica_groups=mesh['zl'=2,'y'=8,'x'=4,'zh'=4,'core'=2] {'x'}, dimensions={0} | all-to-all | bytes 4194304 | tf_op jit(solution)/shard_map/all_to_all | solution.py:20
  88.3 1.5 broadcast_in_dim.29
  89.8 4.5 %all-to-all-start.1 = ((bf16[4,512,512]{2,1,0:T(8,128)(2,1)}), bf16[4,512,512]{2,1,0:T(8,128)(2,1)}, u32[]{:S(2)}, u32[]{:S(2)}) async-start(bf16[4,512,512]{2,1,0:T(8,128)(2,1)} %broadcast_in_dim.29), calls=%async_computation.1 | async-start | bytes 4194304 | tf_op jit(solution)/shard_map/all_to_all | solution.py:20
  94.2 1.3 reduce_sum.33
  95.5 19.2 %all-to-all-done.1 = bf16[4,512,512]{2,1,0:T(8,128)(2,1)} async-done(((bf16[4,512,512]{2,1,0:T(8,128)(2,1)}), bf16[4,512,512]{2,1,0:T(8,128)(2,1)}, u32[]{:S(2)}, u32[]{:S(2)}) %all-to-all-start.1) | async-done | bytes 2097184 | tf_op jit(solution)/shard_map/all_to_all | solution.py:20
  114.6 9.7 %all-to-all-start.3 = ((bf16[4,128,512]{2,1,0:T(8,128)(2,1)}), bf16[4,128,512]{2,1,0:T(8,128)(2,1)S(1)}, u32[]{:S(2)}, u32[]{:S(2)}) async-start(bf16[4,128,512]{2,1,0:T(8,128)(2,1)} %bitcast.6), calls=%async_computation.3 | async-start | bytes 1048576 | tf_op jit(solution)/shard_map/all_to_all | solution.py:20
  124.4 0.0 copy-start.7
  124.4 2.7 %fusion.15 = f32[256,512]{1,0:T(8,128)S(1)} fusion(bf16[256,2048]{1,0:T(8,128)(2,1)} %collective-permute-done, bf16[2048,512]{1,0:T(8,128)(2,1)} %bitcast.2), kind=kOutput, calls=%fused_computation.62 | convolution fusion | flops 536870912 | bytes 3670016 | tf_op jit(solution)/shard_map/dot_general | solution.py:78
  127.1 1.9 %collective-permute-start.1 = (f32[256,512]{1,0:T(8,128)S(1)}, f32[256,512]{1,0:T(8,128)S(1)}, u32[]{:S(2)}, u32[]{:S(2)}) collective-permute-start(f32[256,512]{1,0:T(8,128)S(1)} %fusion.15), channel_id=1, source_target_pairs={{0,1},{1,0},{2,3},{3,2},{4,5},{5,4},{6,7},{7,6},{8,9},{9,8},{10,11... | collective-permute-start | bytes 1572872 | tf_op jit(solution)/shard_map/ppermute | solution.py:33
  129.0 0.0 copy-done.7
  129.0 2.3 %fusion.14 = f32[256,512]{1,0:T(8,128)S(1)} fusion(bf16[256,2048]{1,0:T(8,128)(2,1)S(1)} %copy-done.7, bf16[2048,512]{1,0:T(8,128)(2,1)} %bitcast.2), kind=kOutput, calls=%fused_computation.61 | convolution fusion | flops 536870912 | bytes 3670016 | tf_op jit(solution)/shard_map/dot_general | solution.py:79
  131.3 0.0 copy-start.1
  131.3 0.0 copy-start.2
  131.4 0.0 copy-start.4
  131.4 0.0 copy-start.5
  131.4 0.0 collective-permute-done.1
  131.4 0.8 multiply_convert_fusion
  132.2 3.3 %all-to-all-done.3 = bf16[4,128,512]{2,1,0:T(8,128)(2,1)S(1)} async-done(((bf16[4,128,512]{2,1,0:T(8,128)(2,1)}), bf16[4,128,512]{2,1,0:T(8,128)(2,1)S(1)}, u32[]{:S(2)}, u32[]{:S(2)}) %all-to-all-start.3) | async-done | bytes 524320 | tf_op jit(solution)/shard_map/all_to_all | solution.py:20
  135.5 0.7 broadcast_in_dim.30
  136.1 9.7 %all-to-all-start.5 = ((bf16[16,8,512]{2,1,0:T(8,128)(2,1)}), bf16[16,8,512]{2,1,0:T(8,128)(2,1)S(1)}, u32[]{:S(2)}, u32[]{:S(2)}) async-start(bf16[16,8,512]{2,1,0:T(8,128)(2,1)} %broadcast_in_dim.30), calls=%async_computation.5 | async-start | bytes 262144 | tf_op jit(solution)/shard_map/all_to_all | solution.py:20
  145.8 0.1 convert_reduce_fusion
  145.9 0.0 copy-done.1
  145.9 0.0 copy-done.2
  145.9 0.9 bitcast_add_fusion
  146.8 7.0 %all-to-all-done.5 = bf16[16,8,512]{2,1,0:T(8,128)(2,1)S(1)} async-done(((bf16[16,8,512]{2,1,0:T(8,128)(2,1)}), bf16[16,8,512]{2,1,0:T(8,128)(2,1)S(1)}, u32[]{:S(2)}, u32[]{:S(2)}) %all-to-all-start.5) | async-done | bytes 131104 | tf_op jit(solution)/shard_map/all_to_all | solution.py:20
  153.8 0.0 copy-done.4
  153.8 0.0 copy-done.5
  153.8 1.0 multiply_bitcast_fusion
  (2 shorter events, 0.0 us)
Async XLA Ops:
  0.6 9.9 %copy-start = (bf16[256,4096]{1,0:T(8,128)(2,1)S(1)}, bf16[256,4096]{1,0:T(8,128)(2,1)}, u32[]{:S(2)}) copy-start(bf16[256,4096]{1,0:T(8,128)(2,1)} %param.7) | copy-start | bytes 6291460
  8.8 11.4 %copy-start.3 = (f32[1,128,512]{2,1,0:T(8,128)S(1)}, f32[1,128,512]{2,1,0:T(8,128)}, u32[]{:S(2)}) copy-start(f32[1,128,512]{2,1,0:T(8,128)} %param.9) | copy-start | bytes 786436
  14.6 33.6 %copy-start.8 = (bf16[256,512]{1,0:T(8,128)(2,1)S(1)}, bf16[256,512]{1,0:T(8,128)(2,1)}, u32[]{:S(2)}) copy-start(bf16[256,512]{1,0:T(8,128)(2,1)} %param.8) | copy-start | bytes 786436
  17.4 1.0 copy-start.6
  18.3 33.3 %collective-permute-start = (bf16[256,2048]{1,0:T(8,128)(2,1)}, bf16[256,2048]{1,0:T(8,128)(2,1)}, u32[]{:S(2)}, u32[]{:S(2)}) collective-permute-start(bf16[256,2048]{1,0:T(8,128)(2,1)} %get-tuple-element.9), channel_id=1, source_target_pairs={{0,1},{1,0},{2,3},{3,2},{4,5},{5,4},{6,7},{7,6},{8,9},{9,8},{10,11... | collective-permute-start | bytes 3145736 | tf_op jit(solution)/shard_map/ppermute | solution.py:33
  38.8 23.9 %all-to-all-start = ((bf16[4,128,512]{2,1,0:T(8,128)(2,1)}), bf16[4,128,512]{2,1,0:T(8,128)(2,1)S(1)}, u32[]{:S(2)}, u32[]{:S(2)}) async-start(bf16[4,128,512]{2,1,0:T(8,128)(2,1)} %broadcast_in_dim.13), calls=%async_computation | async-start | bytes 1048576 | tf_op jit(solution)/shard_map/all_to_all | solution.py:20
  48.2 3.4 %collective-permute-start.2 = (bf16[256,512]{1,0:T(8,128)(2,1)S(1)}, bf16[256,512]{1,0:T(8,128)(2,1)S(1)}, u32[]{:S(2)}, u32[]{:S(2)}) collective-permute-start(bf16[256,512]{1,0:T(8,128)(2,1)S(1)} %copy-done.8), channel_id=1, source_target_pairs={{0,1},{1,0},{2,3},{3,2},{4,5},{5,4},{6,7},{7,6},{8,9},{9,8},{10,11... | collective-permute-start | bytes 786440 | tf_op jit(solution)/shard_map/ppermute | solution.py:33
  89.8 24.9 %all-to-all-start.1 = ((bf16[4,512,512]{2,1,0:T(8,128)(2,1)}), bf16[4,512,512]{2,1,0:T(8,128)(2,1)}, u32[]{:S(2)}, u32[]{:S(2)}) async-start(bf16[4,512,512]{2,1,0:T(8,128)(2,1)} %broadcast_in_dim.29), calls=%async_computation.1 | async-start | bytes 4194304 | tf_op jit(solution)/shard_map/all_to_all | solution.py:20
  114.6 20.8 %all-to-all-start.3 = ((bf16[4,128,512]{2,1,0:T(8,128)(2,1)}), bf16[4,128,512]{2,1,0:T(8,128)(2,1)S(1)}, u32[]{:S(2)}, u32[]{:S(2)}) async-start(bf16[4,128,512]{2,1,0:T(8,128)(2,1)} %bitcast.6), calls=%async_computation.3 | async-start | bytes 1048576 | tf_op jit(solution)/shard_map/all_to_all | solution.py:20
  124.4 4.7 %copy-start.7 = (bf16[256,2048]{1,0:T(8,128)(2,1)S(1)}, bf16[256,2048]{1,0:T(8,128)(2,1)}, u32[]{:S(2)}) copy-start(bf16[256,2048]{1,0:T(8,128)(2,1)} %constant_dynamic-update-slice_fusion) | copy-start | bytes 3145732
  127.1 4.3 %collective-permute-start.1 = (f32[256,512]{1,0:T(8,128)S(1)}, f32[256,512]{1,0:T(8,128)S(1)}, u32[]{:S(2)}, u32[]{:S(2)}) collective-permute-start(f32[256,512]{1,0:T(8,128)S(1)} %fusion.15), channel_id=1, source_target_pairs={{0,1},{1,0},{2,3},{3,2},{4,5},{5,4},{6,7},{7,6},{8,9},{9,8},{10,11... | collective-permute-start | bytes 1572872 | tf_op jit(solution)/shard_map/ppermute | solution.py:33
  131.3 14.5 %copy-start.1 = (f32[1,128,512]{2,1,0:T(8,128)S(1)}, f32[1,128,512]{2,1,0:T(8,128)}, u32[]{:S(2)}) copy-start(f32[1,128,512]{2,1,0:T(8,128)} %param.11) | copy-start | bytes 786436
  131.3 14.5 %copy-start.2 = (f32[1,128,512]{2,1,0:T(8,128)S(1)}, f32[1,128,512]{2,1,0:T(8,128)}, u32[]{:S(2)}) copy-start(f32[1,128,512]{2,1,0:T(8,128)} %param.10) | copy-start | bytes 786436
  131.4 22.5 %copy-start.4 = (f32[128,512]{1,0:T(8,128)S(1)}, f32[128,512]{1,0:T(8,128)}, u32[]{:S(2)}) copy-start(f32[128,512]{1,0:T(8,128)} %param.12) | copy-start | bytes 786436
  131.4 22.4 %copy-start.5 = (f32[128,512]{1,0:T(8,128)S(1)}, f32[128,512]{1,0:T(8,128)}, u32[]{:S(2)}) copy-start(f32[128,512]{1,0:T(8,128)} %param.13) | copy-start | bytes 786436
  136.1 17.7 %all-to-all-start.5 = ((bf16[16,8,512]{2,1,0:T(8,128)(2,1)}), bf16[16,8,512]{2,1,0:T(8,128)(2,1)S(1)}, u32[]{:S(2)}, u32[]{:S(2)}) async-start(bf16[16,8,512]{2,1,0:T(8,128)(2,1)} %broadcast_in_dim.30), calls=%async_computation.5 | async-start | bytes 262144 | tf_op jit(solution)/shard_map/all_to_all | solution.py:20

commit v2 on v1

v2 whole, which is shorter than its diff:
```python
import jax
import jax.numpy as jnp
from jax import lax
from jax.experimental import pallas as pl
from jax.experimental.pallas import tpu as pltpu
from jax.sharding import Mesh, PartitionSpec as P

REPLICA = ("zl", "y")
FSDP = ("x", "zh", "core")
F32 = jnp.float32
BF16 = jnp.bfloat16
BLOCK = 128
SMEM = pl.BlockSpec(memory_space=pltpu.SMEM)
VMEM = pl.BlockSpec(memory_space=pltpu.VMEM)


def outer_update(summed, anchor_part, momentum_part, replicas):
    pseudo = anchor_part - summed * (1.0 / replicas)
    momentum_next = 0.9 * momentum_part + pseudo
    anchor_next = anchor_part - 0.7 * (pseudo + 0.9 * momentum_next)
    return (anchor_next, momentum_next)


def trade(block, axis, mask):
    return lax.ppermute(block, axis, [(i, i ^ mask) for i in range(lax.axis_size(axis))])


def add_other(value, axis, mask):
    held = value.astype(BF16)
    return held.astype(F32) + trade(held, axis, mask).astype(F32)


def exchange(blocks, axis):
    return lax.all_to_all(blocks, axis, 0, 0, tiled=True)


def total(blocks):
    return jnp.sum(blocks.astype(F32), axis=0)


def call(kernel, outs, args, flops, name):
    moved = sum(a.size * a.dtype.itemsize for a in args)
    return pl.pallas_call(
        kernel,
        in_specs=[SMEM] + [VMEM] * (len(args) - 1),
        out_specs=[VMEM] * len(outs),
        out_shape=outs,
        cost_estimate=pl.CostEstimate(flops=flops, bytes_accessed=2 * moved, transcendentals=0),
        compiler_params=pltpu.CompilerParams(vmem_limit_bytes=24 * 2**20),
        name=name,
    )(*args)


def send_kernel(place_ref, x_ref, c_ref, out_ref):
    width = x_ref.shape[1]

    def put(offset):
        for block in range(width // (2 * BLOCK)):
            at = 2 * BLOCK * block + offset
            out_ref[:, BLOCK * block : BLOCK * (block + 1)] = x_ref[:, at : at + BLOCK]

    pl.when(place_ref[0] == 0)(lambda: put(BLOCK))
    pl.when(place_ref[0] != 0)(lambda: put(0))
    out_ref[:, width // 2 :] = c_ref[...]


def own_block(core, x_ref, at):
    return x_ref[:, pl.ds(pl.multiple_of((2 * at + core) * BLOCK, BLOCK), BLOCK)]


def their_block(core, got_ref, at):
    return got_ref[:, pl.ds(pl.multiple_of(at * BLOCK, BLOCK), BLOCK)]


def four_blocks(pick, core, ref, j):
    return jnp.concatenate([pick(core, ref, 4 * j + k) for k in range(4)], axis=1)


def grad_kernel(place_ref, x_ref, c_ref, got_ref, out_ref):
    ours = c_ref[...]
    theirs = got_ref[:, got_ref.shape[1] - ours.shape[1] :]
    rows = (((0,), (0,)), ((), ()))
    for j in range(4):
        a = four_blocks(own_block, place_ref[0], x_ref, j)
        b = four_blocks(their_block, place_ref[0], got_ref, j)
        term = lax.dot_general(a, ours, rows, preferred_element_type=F32)
        term += lax.dot_general(b, theirs, rows, preferred_element_type=F32)
        out_ref[j] = term.astype(out_ref.dtype)


def keys_kernel(pick, place_ref, x_ref, *refs):
    out_ref = refs[-1]
    for j, w_ref in enumerate(refs[:-1]):
        group = 4 * (place_ref[1] ^ j)
        picked = [pick(place_ref[0], x_ref, group + (place_ref[2] ^ k)) for k in range(4)]
        a = jnp.concatenate(picked, axis=1)
        term = jnp.dot(a, w_ref[...], preferred_element_type=F32)
        out_ref[...] = term if j == 0 else out_ref[...] + term


def shards(
    activations, cotangent, local_weight, first_moment, second_moment, anchor_weight, outer_momentum
):
    tokens, width = activations.shape
    rows, features = anchor_weight.shape
    scale_factor = width ** (-0.5)
    weight = local_weight[0]
    weight_half = weight.astype(BF16)
    place = jnp.stack([lax.axis_index(a) for a in ("core", "x", "zh")]).astype(jnp.int32)
    keys_shape = jax.ShapeDtypeStruct((tokens, features), F32)
    term_shape = jax.ShapeDtypeStruct((4, 4 * rows, features), BF16)
    sent_shape = jax.ShapeDtypeStruct((tokens, width // 2 + features), BF16)

    sent = call(send_kernel, [sent_shape], (place, activations, cotangent), 0, "send")[0]
    got = trade(sent, "core", 1)

    term = call(
        grad_kernel,
        [term_shape],
        (place, activations, cotangent, got),
        2 * tokens * width * features,
        "grad",
    )[0]
    come = exchange(term, "x")

    late_half = lax.optimization_barrier((weight_half, term))[0]
    near = [late_half] + [trade(late_half, "zh", k) for k in (1, 2, 3)]
    pair = add_other(lax.optimization_barrier((late_half, near[1]))[0], "y", 1)
    column = jnp.concatenate(near, axis=0)
    column, pair = lax.optimization_barrier((column, pair))
    halves = [column] + [trade(column, "x", j) for j in (1, 2, 3)]
    four = add_other(pair, "y", 2)
    eight = add_other(four, "y", 4)
    come, eight = lax.optimization_barrier((come, eight))
    part = total(come).astype(BF16)
    summed = add_other(eight, "zl", 1)

    grad_sum = total(exchange(part.reshape(4, rows, features), "zh"))
    grad = grad_sum * scale_factor

    flops = tokens * width * features

    def their_keys(*refs):
        keys_kernel(their_block, *refs)

    def our_keys(*refs):
        keys_kernel(own_block, *refs)

    halves = lax.optimization_barrier((*halves, part))[:4]
    away = call(their_keys, [keys_shape], (place, got, *halves), flops, "their_keys")[0]
    back = trade(away, "core", 1)
    keys = call(our_keys, [keys_shape], (place, activations, *halves), flops, "our_keys")[0]
    key_out = ((keys + back) * scale_factor).astype(BF16)

    replicas = lax.axis_size(REPLICA)
    new_first = 0.9 * first_moment[0] + 0.1 * grad
    new_second = 0.95 * second_moment[0] + 0.05 * grad * grad
    stepped = weight - 0.02 * (new_first / (jnp.sqrt(new_second) + 1e-08) + 0.1 * weight)
    new_anchor, new_momentum = outer_update(summed, anchor_weight, outer_momentum, replicas)
    new_weight = 0.5 * stepped + 0.5 * new_anchor
    return (key_out, new_weight[None], new_first[None], new_second[None], new_anchor, new_momentum)


def solution(mesh):
    fine = Mesh(mesh.devices.reshape(2, 8, 4, 4, 2), REPLICA + FSDP)
    split = P(REPLICA + FSDP, None)
    state = P(REPLICA, FSDP, None)
    shared = P(FSDP, None)
    return jax.shard_map(
        shards,
        mesh=fine,
        in_specs=(split, split, state, state, state, shared, shared),
        out_specs=(split, state, state, state, shared, shared),
        check_vma=False,
    )
```

time: 156 us -> 99.9 us (0.64)
  the two profiles are of different devices: /device:TPU:8 before, /device:TPU:78 now
where the time goes in v2:
time: 99.9 us; the launch traced here: 99.2 us
  starting transfers between devices  54.7 us (55%)
  waiting for transfers between devices  26.7 us (27%)
  other arithmetic  7.86 us (8%)
  Pallas kernels  6.38 us (6%)
  local copies, waits for them, and re-layouts  2.58 us (3%)
    ppermute x12, starting transfers between devices, trade(): lax.ppermute(block, axis, [(i, i ^ mask) for i in range(lax.axis_size(axi...  43.7 us
    ppermute x12, waiting for transfers between devices, trade(): lax.ppermute(block, axis, [(i, i ^ mask) for i in range(lax.axis_size(axi...  17.2 us
    all_to_all x2, starting transfers between devices, exchange(): return lax.all_to_all(blocks, axis, 0, 0, tiled=True)  11 us
    all_to_all x2, waiting for transfers between devices, exchange(): return lax.all_to_all(blocks, axis, 0, 0, tiled=True)  9.5 us
    pallas_call x4, Pallas kernels, call(): pl.pallas_call(kernel, in_specs=[SMEM] + [VMEM] * (len(args) - 1), out_sp...  6.38 us
    reduce_sum x2, other arithmetic, total(): return jnp.sum(blocks.astype(F32), axis=0)  3.99 us
    unnamed x18, local copies, waits for them, and re-layouts  2.58 us
  transfers between devices with their start and end apart: 14, of which 4 were waited for; matrix products, arithmetic and copies ran while one was open for 6% of the time, Pallas kernels for 3%

profile of v2, /device:TPU:78, one launch (start us, length us, event | category | flops | bytes accessed | tf_op | source)
XLA Modules:
  0.0 99.2 jit_solution(150297753155155962)
XLA Ops:
  0.6 0.1 pad_add_fusion.place_ref.refs_0_
  0.7 0.0 copy-start
  0.7 1.6 %copy-done = bf16[256,4096]{1,0:T(8,128)(2,1)S(1)} copy-done((bf16[256,4096]{1,0:T(8,128)(2,1)S(1)}, bf16[256,4096]{1,0:T(8,128)(2,1)}, u32[]{:S(2)}) %copy-start) | copy-done | bytes 2097176
  2.3 0.0 copy-start.2
  2.3 0.9 copy-done.2
  3.3 0.8 send.1
  4.0 1.9 %collective-permute-start = (bf16[256,2560]{1,0:T(8,128)(2,1)S(1)}, bf16[256,2560]{1,0:T(8,128)(2,1)S(1)}, u32[]{:S(2)}, u32[]{:S(2)}) collective-permute-start(bf16[256,2560]{1,0:T(8,128)(2,1)S(1)} %send.1), channel_id=1, source_target_pairs={{0,1},{1,0},{2,3},{3,2},{4,5},{5,4},{6,7},{7,6},{8,9},{9,8},{10,11... | collective-permute-start | bytes 3932168 | tf_op jit(solution)/shard_map/ppermute | solution.py:25
  5.9 3.0 %collective-permute-done.got_ref.refs_1_ = bf16[256,2560]{1,0:T(8,128)(2,1)S(1)} collective-permute-done((bf16[256,2560]{1,0:T(8,128)(2,1)S(1)}, bf16[256,2560]{1,0:T(8,128)(2,1)S(1)}, u32[]{:S(2)}, u32[]{:S(2)}) %collective-permute-start) | collective-permute-done | bytes 1310752 | tf_op jit(solution)/shard_map/ppermute | solution.py:25
  8.9 3.1 %grad.1 = bf16[4,512,512]{2,1,0:T(8,128)(2,1)} custom-call(s32[3]{0:T(128)S(1)} %pad_add_fusion.place_ref.refs_0_, bf16[256,4096]{1,0:T(8,128)(2,1)S(1)} %copy-done, bf16[256,512]{1,0:T(8,128)(2,1)S(1)} %copy-done.2, bf16[256,2560]{1,0:T(8,128)(2,1)S(1)} %collective-permute-done.got_ref.refs_1_), custom_call_target="tpu_custom_call" | custom-call | flops 1073741824 | bytes 7340056 | tf_op jit(solution)/shard_map/grad/pallas_call | solution.py:43
  12.1 0.0 copy-start.5
  12.1 5.0 %all-to-all-start = ((bf16[4,512,512]{2,1,0:T(8,128)(2,1)}), bf16[4,512,512]{2,1,0:T(8,128)(2,1)}, u32[]{:S(2)}, u32[]{:S(2)}) async-start(bf16[4,512,512]{2,1,0:T(8,128)(2,1)} %grad.1), calls=%async_computation | async-start | bytes 4194304 | tf_op jit(solution)/shard_map/all_to_all | solution.py:34
  17.1 0.0 copy-done.5
  17.1 6.1 %collective-permute-start.1 = (bf16[128,512]{1,0:T(8,128)(2,1)S(1)}, bf16[128,512]{1,0:T(8,128)(2,1)S(1)}, u32[]{:S(2)}, u32[]{:S(2)}) collective-permute-start(bf16[128,512]{1,0:T(8,128)(2,1)S(1)} %bitcast_convert_fusion), channel_id=1, source_target_pairs={{0,2},{2,0},{4,6},{6,4},{1,3},{3,1},{5,7},{7,5},{8,10},{10,8},{12,... | collective-permute-start | bytes 393224 | tf_op jit(solution)/shard_map/ppermute | solution.py:25
  23.2 6.4 %collective-permute-start.3 = (bf16[128,512]{1,0:T(8,128)(2,1)S(1)}, bf16[128,512]{1,0:T(8,128)(2,1)S(1)}, u32[]{:S(2)}, u32[]{:S(2)}) collective-permute-start(bf16[128,512]{1,0:T(8,128)(2,1)S(1)} %bitcast_convert_fusion), channel_id=1, source_target_pairs={{0,6},{2,4},{4,2},{6,0},{1,7},{3,5},{5,3},{7,1},{8,14},{10,12},{12... | collective-permute-start | bytes 393224 | tf_op jit(solution)/shard_map/ppermute | solution.py:25
  29.6 3.7 %collective-permute-start.2 = (bf16[128,512]{1,0:T(8,128)(2,1)S(1)}, bf16[128,512]{1,0:T(8,128)(2,1)S(1)}, u32[]{:S(2)}, u32[]{:S(2)}) collective-permute-start(bf16[128,512]{1,0:T(8,128)(2,1)S(1)} %bitcast_convert_fusion), channel_id=1, source_target_pairs={{0,4},{2,6},{4,0},{6,2},{1,5},{3,7},{5,1},{7,3},{8,12},{10,14},{12... | collective-permute-start | bytes 393224 | tf_op jit(solution)/shard_map/ppermute | solution.py:25
  33.4 0.0 collective-permute-done.1
  33.4 2.4 %collective-permute-start.4 = (bf16[128,512]{1,0:T(8,128)(2,1)S(1)}, bf16[128,512]{1,0:T(8,128)(2,1)S(1)}, u32[]{:S(2)}, u32[]{:S(2)}) collective-permute-start(bf16[128,512]{1,0:T(8,128)(2,1)S(1)} %bitcast_convert_fusion), channel_id=1, source_target_pairs={{0,32},{32,0},{64,96},{96,64},{128,160},{160,128},{192,224},{224,1... | collective-permute-start | bytes 393224 | tf_op jit(solution)/shard_map/ppermute | solution.py:25
  35.8 0.0 collective-permute-done.3
  35.8 7.3 %collective-permute-done.2 = bf16[128,512]{1,0:T(8,128)(2,1)S(1)} collective-permute-done((bf16[128,512]{1,0:T(8,128)(2,1)S(1)}, bf16[128,512]{1,0:T(8,128)(2,1)S(1)}, u32[]{:S(2)}, u32[]{:S(2)}) %collective-permute-start.2) | collective-permute-done | bytes 131104 | tf_op jit(solution)/shard_map/ppermute | solution.py:25
  43.1 0.0 collective-permute-done.4
  43.2 4.5 %collective-permute-start.8 = (bf16[128,512]{1,0:T(8,128)(2,1)S(1)}, bf16[128,512]{1,0:T(8,128)(2,1)S(1)}, u32[]{:S(2)}, u32[]{:S(2)}) collective-permute-start(bf16[128,512]{1,0:T(8,128)(2,1)S(1)} %convert_add_fusion.1), channel_id=1, source_target_pairs={{0,64},{32,96},{64,0},{96,32},{128,192},{160,224},{192,128},{224,1... | collective-permute-start | bytes 393224 | tf_op jit(solution)/shard_map/ppermute | solution.py:25
  47.7 2.0 %collective-permute-start.7 = (bf16[512,512]{1,0:T(8,128)(2,1)S(1)}, bf16[512,512]{1,0:T(8,128)(2,1)S(1)}, u32[]{:S(2)}, u32[]{:S(2)}) collective-permute-start(bf16[512,512]{1,0:T(8,128)(2,1)S(1)} %pad_maximum_fusion.refs_2_), channel_id=1, source_target_pairs={{0,24},{8,16},{16,8},{24,0},{1,25},{9,17},{17,9},{25,1},{2,26},{10... | collective-permute-start | bytes 1572872 | tf_op jit(solution)/shard_map/ppermute | solution.py:25
  49.7 4.8 %collective-permute-start.6 = (bf16[512,512]{1,0:T(8,128)(2,1)S(1)}, bf16[512,512]{1,0:T(8,128)(2,1)S(1)}, u32[]{:S(2)}, u32[]{:S(2)}) collective-permute-start(bf16[512,512]{1,0:T(8,128)(2,1)S(1)} %pad_maximum_fusion.refs_2_), channel_id=1, source_target_pairs={{0,16},{8,24},{16,0},{24,8},{1,17},{9,25},{17,1},{25,9},{2,18},{10... | collective-permute-start | bytes 1572872 | tf_op jit(solution)/shard_map/ppermute | solution.py:25
  54.4 3.1 %collective-permute-start.5 = (bf16[512,512]{1,0:T(8,128)(2,1)S(1)}, bf16[512,512]{1,0:T(8,128)(2,1)S(1)}, u32[]{:S(2)}, u32[]{:S(2)}) collective-permute-start(bf16[512,512]{1,0:T(8,128)(2,1)S(1)} %pad_maximum_fusion.refs_2_), channel_id=1, source_target_pairs={{0,8},{8,0},{16,24},{24,16},{1,9},{9,1},{17,25},{25,17},{2,10},{10... | collective-permute-start | bytes 1572872 | tf_op jit(solution)/shard_map/ppermute | solution.py:25
  57.5 0.0 collective-permute-done.8
  57.6 5.0 %collective-permute-start.9 = (bf16[128,512]{1,0:T(8,128)(2,1)S(1)}, bf16[128,512]{1,0:T(8,128)(2,1)S(1)}, u32[]{:S(2)}, u32[]{:S(2)}) collective-permute-start(bf16[128,512]{1,0:T(8,128)(2,1)S(1)} %add_convert_fusion), channel_id=1, source_target_pairs={{0,128},{32,160},{64,192},{96,224},{128,0},{160,32},{192,64},{224,... | collective-permute-start | bytes 393224 | tf_op jit(solution)/shard_map/ppermute | solution.py:25
  62.6 6.9 %collective-permute-done.9 = bf16[128,512]{1,0:T(8,128)(2,1)S(1)} collective-permute-done((bf16[128,512]{1,0:T(8,128)(2,1)S(1)}, bf16[128,512]{1,0:T(8,128)(2,1)S(1)}, u32[]{:S(2)}, u32[]{:S(2)}) %collective-permute-start.9) | collective-permute-done | bytes 131104 | tf_op jit(solution)/shard_map/ppermute | solution.py:25
  69.6 0.0 all-to-all-done
  69.6 2.8 %reduce_sum.21 = bf16[512,512]{1,0:T(8,128)(2,1)} reduce(bf16[4,512,512]{2,1,0:T(8,128)(2,1)} %all-to-all-done, bf16[]{:T(256)} %constant.9.clone.1), dimensions={0}, to_apply=%region_0.0 | reduce | flops 786432 | bytes 2621442 | tf_op jit(solution)/shard_map/reduce_sum | solution.py:38
  72.4 6.0 %all-to-all-start.1 = ((bf16[4,128,512]{2,1,0:T(8,128)(2,1)}), bf16[4,128,512]{2,1,0:T(8,128)(2,1)}, u32[]{:S(2)}, u32[]{:S(2)}) async-start(bf16[4,128,512]{2,1,0:T(8,128)(2,1)} %bitcast.42), calls=%async_computation.1 | async-start | bytes 1048576 | tf_op jit(solution)/shard_map/all_to_all | solution.py:34
  78.4 0.0 copy-start.1
  78.4 0.0 collective-permute-done.7.refs_5_
  78.4 0.0 collective-permute-done.6.refs_4_
  78.4 0.0 collective-permute-done.5.refs_3_
  78.4 1.2 %their_keys.1 = f32[256,512]{1,0:T(8,128)S(1)} custom-call(s32[3]{0:T(128)S(1)} %pad_add_fusion.place_ref.refs_0_, bf16[256,2560]{1,0:T(8,128)(2,1)S(1)} %collective-permute-done.got_ref.refs_1_, bf16[512,512]{1,0:T(8,128)(2,1)S(1)} %pad_maximum_fusion.refs_2_, bf16[512,512]{1,0:T(8,128)(2,1)S(1)} %collective-permute-done.5.refs_3_, ...), custom_call_target="tpu_custom_call" | custom-call | flops 536870912 | bytes 6815768 | tf_op jit(solution)/shard_map/their_keys/pallas_call | solution.py:43
  79.7 1.9 %collective-permute-start.10 = (f32[256,512]{1,0:T(8,128)S(1)}, f32[256,512]{1,0:T(8,128)S(1)}, u32[]{:S(2)}, u32[]{:S(2)}) collective-permute-start(f32[256,512]{1,0:T(8,128)S(1)} %their_keys.1), channel_id=1, source_target_pairs={{0,1},{1,0},{2,3},{3,2},{4,5},{5,4},{6,7},{7,6},{8,9},{9,8},{10,11... | collective-permute-start | bytes 1572872 | tf_op jit(solution)/shard_map/ppermute | solution.py:25
  81.6 1.9 %collective-permute-start.11 = (bf16[128,512]{1,0:T(8,128)(2,1)S(1)}, bf16[128,512]{1,0:T(8,128)(2,1)}, u32[]{:S(2)}, u32[]{:S(2)}) collective-permute-start(bf16[128,512]{1,0:T(8,128)(2,1)S(1)} %convert_add_fusion), channel_id=1, source_target_pairs={{0,256},{256,0},{1,257},{257,1},{2,258},{258,2},{3,259},{259,3},{4... | collective-permute-start | bytes 393224 | tf_op jit(solution)/shard_map/ppermute | solution.py:25
  83.5 0.0 copy-done.1
  83.5 1.2 %our_keys.1 = f32[256,512]{1,0:T(8,128)S(1)} custom-call(s32[3]{0:T(128)S(1)} %pad_add_fusion.place_ref.refs_0_, bf16[256,4096]{1,0:T(8,128)(2,1)S(1)} %copy-done.1, bf16[512,512]{1,0:T(8,128)(2,1)S(1)} %pad_maximum_fusion.refs_2_, bf16[512,512]{1,0:T(8,128)(2,1)S(1)} %collective-permute-done.5.refs_3_, bf16[512,512]{1,0:T(8,128)(2,1)S(1)} %collective-permute-done.6.refs_4_, ...), custom_call_target="tpu_custom_call" | custom-call | flops 536870912 | bytes 8388632 | tf_op jit(solution)/shard_map/our_keys/pallas_call | solution.py:43
  84.8 0.0 copy-start.3
  84.8 0.0 copy-start.4
  84.8 0.0 copy-start.6
  84.8 0.0 copy-start.7
  84.8 0.0 copy-start.8
  84.9 0.0 collective-permute-done.10
  84.9 0.8 multiply_convert_fusion
  85.7 9.5 %all-to-all-done.1 = bf16[4,128,512]{2,1,0:T(8,128)(2,1)} async-done(((bf16[4,128,512]{2,1,0:T(8,128)(2,1)}), bf16[4,128,512]{2,1,0:T(8,128)(2,1)}, u32[]{:S(2)}, u32[]{:S(2)}) %all-to-all-start.1) | async-done | bytes 524320 | tf_op jit(solution)/shard_map/all_to_all | solution.py:34
  95.2 1.1 %convert_reduce_fusion = f32[128,512]{1,0:T(8,128)S(1)} fusion(bf16[4,128,512]{2,1,0:T(8,128)(2,1)} %all-to-all-done.1), kind=kLoop, calls=%fused_computation | loop fusion | flops 458752 | bytes 786432 | tf_op jit(solution)/shard_map/reduce_sum | solution.py:38
  96.3 0.0 copy-done.3
  96.3 0.0 copy-done.4
  96.4 0.9 bitcast_add_fusion
  97.2 0.0 collective-permute-done.11
  97.2 0.0 copy-done.6
  97.2 0.0 copy-done.7
  97.3 0.0 copy-done.8
  97.3 1.9 %multiply_bitcast_fusion = (f32[1,128,512]{2,1,0:T(8,128)}, f32[128,512]{1,0:T(8,128)}, f32[128,512]{1,0:T(8,128)}) fusion(f32[1,128,512]{2,1,0:T(8,128)S(1)} %copy-done.6, f32[1,128,512]{2,1,0:T(8,128)S(1)} %copy-done.3, f32[128,512]{1,0:T(8,128)S(1)} %convert_reduce_fusion, f32[1,128,512]{2,1,0:T(8,128)S(1)} %copy-done.4, f32[128,512]{1,0:T(8,128)S(1)} %copy-done.7, ...), kind=kLoop, calls=%fused_computation.16 | loop fusion | flops 1769472 | bytes 2621440 | tf_op jit(solution)/shard_map/broadcast_in_dim | solution.py:161
  (5 shorter events, 0.2 us)
Async XLA Ops:
  0.7 1.6 %copy-start = (bf16[256,4096]{1,0:T(8,128)(2,1)S(1)}, bf16[256,4096]{1,0:T(8,128)(2,1)}, u32[]{:S(2)}) copy-start(bf16[256,4096]{1,0:T(8,128)(2,1)} %refs_1_.1) | copy-start | bytes 6291460
  2.3 0.9 copy-start.2
  4.0 4.9 %collective-permute-start = (bf16[256,2560]{1,0:T(8,128)(2,1)S(1)}, bf16[256,2560]{1,0:T(8,128)(2,1)S(1)}, u32[]{:S(2)}, u32[]{:S(2)}) collective-permute-start(bf16[256,2560]{1,0:T(8,128)(2,1)S(1)} %send.1), channel_id=1, source_target_pairs={{0,1},{1,0},{2,3},{3,2},{4,5},{5,4},{6,7},{7,6},{8,9},{9,8},{10,11... | collective-permute-start | bytes 3932168 | tf_op jit(solution)/shard_map/ppermute | solution.py:25
  12.1 5.0 %copy-start.5 = (f32[1,128,512]{2,1,0:T(8,128)S(1)}, f32[1,128,512]{2,1,0:T(8,128)}, u32[]{:S(2)}) copy-start(f32[1,128,512]{2,1,0:T(8,128)} %param.9) | copy-start | bytes 786436
  12.1 57.5 %all-to-all-start = ((bf16[4,512,512]{2,1,0:T(8,128)(2,1)}), bf16[4,512,512]{2,1,0:T(8,128)(2,1)}, u32[]{:S(2)}, u32[]{:S(2)}) async-start(bf16[4,512,512]{2,1,0:T(8,128)(2,1)} %grad.1), calls=%async_computation | async-start | bytes 4194304 | tf_op jit(solution)/shard_map/all_to_all | solution.py:34
  17.1 16.3 %collective-permute-start.1 = (bf16[128,512]{1,0:T(8,128)(2,1)S(1)}, bf16[128,512]{1,0:T(8,128)(2,1)S(1)}, u32[]{:S(2)}, u32[]{:S(2)}) collective-permute-start(bf16[128,512]{1,0:T(8,128)(2,1)S(1)} %bitcast_convert_fusion), channel_id=1, source_target_pairs={{0,2},{2,0},{4,6},{6,4},{1,3},{3,1},{5,7},{7,5},{8,10},{10,8},{12,... | collective-permute-start | bytes 393224 | tf_op jit(solution)/shard_map/ppermute | solution.py:25
  23.2 12.5 %collective-permute-start.3 = (bf16[128,512]{1,0:T(8,128)(2,1)S(1)}, bf16[128,512]{1,0:T(8,128)(2,1)S(1)}, u32[]{:S(2)}, u32[]{:S(2)}) collective-permute-start(bf16[128,512]{1,0:T(8,128)(2,1)S(1)} %bitcast_convert_fusion), channel_id=1, source_target_pairs={{0,6},{2,4},{4,2},{6,0},{1,7},{3,5},{5,3},{7,1},{8,14},{10,12},{12... | collective-permute-start | bytes 393224 | tf_op jit(solution)/shard_map/ppermute | solution.py:25
  29.6 13.4 %collective-permute-start.2 = (bf16[128,512]{1,0:T(8,128)(2,1)S(1)}, bf16[128,512]{1,0:T(8,128)(2,1)S(1)}, u32[]{:S(2)}, u32[]{:S(2)}) collective-permute-start(bf16[128,512]{1,0:T(8,128)(2,1)S(1)} %bitcast_convert_fusion), channel_id=1, source_target_pairs={{0,4},{2,6},{4,0},{6,2},{1,5},{3,7},{5,1},{7,3},{8,12},{10,14},{12... | collective-permute-start | bytes 393224 | tf_op jit(solution)/shard_map/ppermute | solution.py:25
  33.4 9.7 %collective-permute-start.4 = (bf16[128,512]{1,0:T(8,128)(2,1)S(1)}, bf16[128,512]{1,0:T(8,128)(2,1)S(1)}, u32[]{:S(2)}, u32[]{:S(2)}) collective-permute-start(bf16[128,512]{1,0:T(8,128)(2,1)S(1)} %bitcast_convert_fusion), channel_id=1, source_target_pairs={{0,32},{32,0},{64,96},{96,64},{128,160},{160,128},{192,224},{224,1... | collective-permute-start | bytes 393224 | tf_op jit(solution)/shard_map/ppermute | solution.py:25
  43.2 14.3 %collective-permute-start.8 = (bf16[128,512]{1,0:T(8,128)(2,1)S(1)}, bf16[128,512]{1,0:T(8,128)(2,1)S(1)}, u32[]{:S(2)}, u32[]{:S(2)}) collective-permute-start(bf16[128,512]{1,0:T(8,128)(2,1)S(1)} %convert_add_fusion.1), channel_id=1, source_target_pairs={{0,64},{32,96},{64,0},{96,32},{128,192},{160,224},{192,128},{224,1... | collective-permute-start | bytes 393224 | tf_op jit(solution)/shard_map/ppermute | solution.py:25
  47.7 30.7 %collective-permute-start.7 = (bf16[512,512]{1,0:T(8,128)(2,1)S(1)}, bf16[512,512]{1,0:T(8,128)(2,1)S(1)}, u32[]{:S(2)}, u32[]{:S(2)}) collective-permute-start(bf16[512,512]{1,0:T(8,128)(2,1)S(1)} %pad_maximum_fusion.refs_2_), channel_id=1, source_target_pairs={{0,24},{8,16},{16,8},{24,0},{1,25},{9,17},{17,9},{25,1},{2,26},{10... | collective-permute-start | bytes 1572872 | tf_op jit(solution)/shard_map/ppermute | solution.py:25
  49.7 28.7 %collective-permute-start.6 = (bf16[512,512]{1,0:T(8,128)(2,1)S(1)}, bf16[512,512]{1,0:T(8,128)(2,1)S(1)}, u32[]{:S(2)}, u32[]{:S(2)}) collective-permute-start(bf16[512,512]{1,0:T(8,128)(2,1)S(1)} %pad_maximum_fusion.refs_2_), channel_id=1, source_target_pairs={{0,16},{8,24},{16,0},{24,8},{1,17},{9,25},{17,1},{25,9},{2,18},{10... | collective-permute-start | bytes 1572872 | tf_op jit(solution)/shard_map/ppermute | solution.py:25
  54.4 24.0 %collective-permute-start.5 = (bf16[512,512]{1,0:T(8,128)(2,1)S(1)}, bf16[512,512]{1,0:T(8,128)(2,1)S(1)}, u32[]{:S(2)}, u32[]{:S(2)}) collective-permute-start(bf16[512,512]{1,0:T(8,128)(2,1)S(1)} %pad_maximum_fusion.refs_2_), channel_id=1, source_target_pairs={{0,8},{8,0},{16,24},{24,16},{1,9},{9,1},{17,25},{25,17},{2,10},{10... | collective-permute-start | bytes 1572872 | tf_op jit(solution)/shard_map/ppermute | solution.py:25
  57.6 11.9 %collective-permute-start.9 = (bf16[128,512]{1,0:T(8,128)(2,1)S(1)}, bf16[128,512]{1,0:T(8,128)(2,1)S(1)}, u32[]{:S(2)}, u32[]{:S(2)}) collective-permute-start(bf16[128,512]{1,0:T(8,128)(2,1)S(1)} %add_convert_fusion), channel_id=1, source_target_pairs={{0,128},{32,160},{64,192},{96,224},{128,0},{160,32},{192,64},{224,... | collective-permute-start | bytes 393224 | tf_op jit(solution)/shard_map/ppermute | solution.py:25
  72.4 22.8 %all-to-all-start.1 = ((bf16[4,128,512]{2,1,0:T(8,128)(2,1)}), bf16[4,128,512]{2,1,0:T(8,128)(2,1)}, u32[]{:S(2)}, u32[]{:S(2)}) async-start(bf16[4,128,512]{2,1,0:T(8,128)(2,1)} %bitcast.42), calls=%async_computation.1 | async-start | bytes 1048576 | tf_op jit(solution)/shard_map/all_to_all | solution.py:34
  78.4 5.1 %copy-start.1 = (bf16[256,4096]{1,0:T(8,128)(2,1)S(1)}, bf16[256,4096]{1,0:T(8,128)(2,1)}, u32[]{:S(2)}) copy-start(bf16[256,4096]{1,0:T(8,128)(2,1)} %refs_1_.1) | copy-start | bytes 6291460
  79.7 5.2 %collective-permute-start.10 = (f32[256,512]{1,0:T(8,128)S(1)}, f32[256,512]{1,0:T(8,128)S(1)}, u32[]{:S(2)}, u32[]{:S(2)}) collective-permute-start(f32[256,512]{1,0:T(8,128)S(1)} %their_keys.1), channel_id=1, source_target_pairs={{0,1},{1,0},{2,3},{3,2},{4,5},{5,4},{6,7},{7,6},{8,9},{9,8},{10,11... | collective-permute-start | bytes 1572872 | tf_op jit(solution)/shard_map/ppermute | solution.py:25
  81.6 15.6 %collective-permute-start.11 = (bf16[128,512]{1,0:T(8,128)(2,1)S(1)}, bf16[128,512]{1,0:T(8,128)(2,1)}, u32[]{:S(2)}, u32[]{:S(2)}) collective-permute-start(bf16[128,512]{1,0:T(8,128)(2,1)S(1)} %convert_add_fusion), channel_id=1, source_target_pairs={{0,256},{256,0},{1,257},{257,1},{2,258},{258,2},{3,259},{259,3},{4... | collective-permute-start | bytes 393224 | tf_op jit(solution)/shard_map/ppermute | solution.py:25
  84.8 11.5 %copy-start.3 = (f32[1,128,512]{2,1,0:T(8,128)S(1)}, f32[1,128,512]{2,1,0:T(8,128)}, u32[]{:S(2)}) copy-start(f32[1,128,512]{2,1,0:T(8,128)} %param.11) | copy-start | bytes 786436
  84.8 11.5 %copy-start.4 = (f32[1,128,512]{2,1,0:T(8,128)S(1)}, f32[1,128,512]{2,1,0:T(8,128)}, u32[]{:S(2)}) copy-start(f32[1,128,512]{2,1,0:T(8,128)} %param.10) | copy-start | bytes 786436
  84.8 12.4 %copy-start.6 = (f32[1,128,512]{2,1,0:T(8,128)S(1)}, f32[1,128,512]{2,1,0:T(8,128)}, u32[]{:S(2)}) copy-start(f32[1,128,512]{2,1,0:T(8,128)} %param.9) | copy-start | bytes 786436
  84.8 12.4 %copy-start.7 = (f32[128,512]{1,0:T(8,128)S(1)}, f32[128,512]{1,0:T(8,128)}, u32[]{:S(2)}) copy-start(f32[128,512]{1,0:T(8,128)} %param.12) | copy-start | bytes 786436
  84.8 12.4 %copy-start.8 = (f32[128,512]{1,0:T(8,128)S(1)}, f32[128,512]{1,0:T(8,128)}, u32[]{:S(2)}) copy-start(f32[128,512]{1,0:T(8,128)} %param.13) | copy-start | bytes 786436

commit v3 on v2

--- a/solution.py
+++ b/solution.py
@@ -38,17 +38,22 @@
     return jnp.sum(blocks.astype(F32), axis=0)
 
 
-def call(kernel, outs, args, flops, name):
+def call(kernel, outs, args, flops, name, after=()):
+    count = len(args)
     moved = sum(a.size * a.dtype.itemsize for a in args)
+
+    def body(*refs):
+        kernel(*refs[:count], *refs[count + len(after) :])
+
     return pl.pallas_call(
-        kernel,
-        in_specs=[SMEM] + [VMEM] * (len(args) - 1),
+        body,
+        in_specs=[SMEM] + [VMEM] * (count - 1) + [pl.BlockSpec(memory_space=pl.ANY)] * len(after),
         out_specs=[VMEM] * len(outs),
         out_shape=outs,
         cost_estimate=pl.CostEstimate(flops=flops, bytes_accessed=2 * moved, transcendentals=0),
         compiler_params=pltpu.CompilerParams(vmem_limit_bytes=24 * 2**20),
         name=name,
-    )(*args)
+    )(*args, *after)
 
 
 def send_kernel(place_ref, x_ref, c_ref, out_ref):
@@ -130,9 +135,9 @@
     column, pair = lax.optimization_barrier((column, pair))
     halves = [column] + [trade(column, "x", j) for j in (1, 2, 3)]
     four = add_other(pair, "y", 2)
+    come, four = lax.optimization_barrier((come, four))
+    part = total(come).astype(BF16)
     eight = add_other(four, "y", 4)
-    come, eight = lax.optimization_barrier((come, eight))
-    part = total(come).astype(BF16)
     summed = add_other(eight, "zl", 1)
 
     grad_sum = total(exchange(part.reshape(4, rows, features), "zh"))
@@ -146,8 +151,7 @@
     def our_keys(*refs):
         keys_kernel(own_block, *refs)
 
-    halves = lax.optimization_barrier((*halves, part))[:4]
-    away = call(their_keys, [keys_shape], (place, got, *halves), flops, "their_keys")[0]
+    away = call(their_keys, [keys_shape], (place, got, *halves), flops, "their_keys", after=(part, eight))[0]
     back = trade(away, "core", 1)
     keys = call(our_keys, [keys_shape], (place, activations, *halves), flops, "our_keys")[0]
     key_out = ((keys + back) * scale_factor).astype(BF16)

time: 99.9 us -> 92.7 us (0.928)
  the two profiles are of different devices: /device:TPU:78 before, /device:TPU:1 now
where the time goes in v3:
time: 92.7 us; the launch traced here: 92 us
  starting transfers between devices  58.9 us (64%)
  waiting for transfers between devices  15.2 us (16%)
  other arithmetic  7.92 us (9%)
  Pallas kernels  6.39 us (7%)
  local copies, waits for them, and re-layouts  2.59 us (3%)
  between operations  0.94 us (1%)
    ppermute x12, starting transfers between devices, trade(): lax.ppermute(block, axis, [(i, i ^ mask) for i in range(lax.axis_size(axi...  48.8 us
    ppermute x12, waiting for transfers between devices, trade(): lax.ppermute(block, axis, [(i, i ^ mask) for i in range(lax.axis_size(axi...  15.2 us
    all_to_all x2, starting transfers between devices, exchange(): return lax.all_to_all(blocks, axis, 0, 0, tiled=True)  10 us
    pallas_call x4, Pallas kernels, call(): pl.pallas_call(body, in_specs=[SMEM] + [VMEM] * (count - 1) + [pl.BlockSp...  6.39 us
    reduce_sum x2, other arithmetic, total(): return jnp.sum(blocks.astype(F32), axis=0)  3.98 us
    unnamed x20, local copies, waits for them, and re-layouts  2.59 us
  transfers between devices with their start and end apart: 14, of which 5 were waited for; matrix products, arithmetic and copies ran while one was open for 7% of the time, Pallas kernels for 3%

profile of v3, /device:TPU:1, one launch (start us, length us, event | category | flops | bytes accessed | tf_op | source)
XLA Modules:
  0.0 92.0 jit_solution(10084995043289597074)
XLA Ops:
  0.6 0.1 pad_add_fusion.refs_0_
  0.7 0.0 copy-start
  0.7 1.6 %copy-done = bf16[256,4096]{1,0:T(8,128)(2,1)S(1)} copy-done((bf16[256,4096]{1,0:T(8,128)(2,1)S(1)}, bf16[256,4096]{1,0:T(8,128)(2,1)}, u32[]{:S(2)}) %copy-start) | copy-done | bytes 2097176
  2.3 0.0 copy-start.2
  2.3 0.9 %copy-done.2 = bf16[256,512]{1,0:T(8,128)(2,1)S(1)} copy-done((bf16[256,512]{1,0:T(8,128)(2,1)S(1)}, bf16[256,512]{1,0:T(8,128)(2,1)}, u32[]{:S(2)}) %copy-start.2) | copy-done | bytes 262168
  3.3 0.8 send.1
  4.0 8.8 %collective-permute-start = (bf16[256,2560]{1,0:T(8,128)(2,1)S(1)}, bf16[256,2560]{1,0:T(8,128)(2,1)S(1)}, u32[]{:S(2)}, u32[]{:S(2)}) collective-permute-start(bf16[256,2560]{1,0:T(8,128)(2,1)S(1)} %send.1), channel_id=1, source_target_pairs={{0,1},{1,0},{2,3},{3,2},{4,5},{5,4},{6,7},{7,6},{8,9},{9,8},{10,11... | collective-permute-start | bytes 3932168 | tf_op jit(solution)/shard_map/ppermute | solution.py:25
  12.8 2.6 %collective-permute-done.refs_3_.refs_1_ = bf16[256,2560]{1,0:T(8,128)(2,1)S(1)} collective-permute-done((bf16[256,2560]{1,0:T(8,128)(2,1)S(1)}, bf16[256,2560]{1,0:T(8,128)(2,1)S(1)}, u32[]{:S(2)}, u32[]{:S(2)}) %collective-permute-start) | collective-permute-done | bytes 1310752 | tf_op jit(solution)/shard_map/ppermute | solution.py:25
  15.5 3.1 %grad.1 = bf16[4,512,512]{2,1,0:T(8,128)(2,1)} custom-call(s32[3]{0:T(128)S(1)} %pad_add_fusion.refs_0_, bf16[256,4096]{1,0:T(8,128)(2,1)S(1)} %copy-done, bf16[256,512]{1,0:T(8,128)(2,1)S(1)} %copy-done.2, bf16[256,2560]{1,0:T(8,128)(2,1)S(1)} %collective-permute-done.refs_3_.refs_1_), custom_call_target="tpu_custom_call" | custom-call | flops 1073741824 | bytes 7340056 | tf_op jit(solution)/shard_map/grad/pallas_call | solution.py:48
  18.6 0.0 copy-start.5
  18.6 4.6 %all-to-all-start = ((bf16[4,512,512]{2,1,0:T(8,128)(2,1)}), bf16[4,512,512]{2,1,0:T(8,128)(2,1)}, u32[]{:S(2)}, u32[]{:S(2)}) async-start(bf16[4,512,512]{2,1,0:T(8,128)(2,1)} %grad.1), calls=%async_computation | async-start | bytes 4194304 | tf_op jit(solution)/shard_map/all_to_all | solution.py:34
  23.2 0.0 copy-done.5
  23.2 1.9 %collective-permute-start.1 = (bf16[128,512]{1,0:T(8,128)(2,1)S(1)}, bf16[128,512]{1,0:T(8,128)(2,1)S(1)}, u32[]{:S(2)}, u32[]{:S(2)}) collective-permute-start(bf16[128,512]{1,0:T(8,128)(2,1)S(1)} %bitcast_convert_fusion), channel_id=1, source_target_pairs={{0,2},{2,0},{4,6},{6,4},{1,3},{3,1},{5,7},{7,5},{8,10},{10,8},{12,... | collective-permute-start | bytes 393224 | tf_op jit(solution)/shard_map/ppermute | solution.py:25
  25.1 5.5 %collective-permute-start.3 = (bf16[128,512]{1,0:T(8,128)(2,1)S(1)}, bf16[128,512]{1,0:T(8,128)(2,1)S(1)}, u32[]{:S(2)}, u32[]{:S(2)}) collective-permute-start(bf16[128,512]{1,0:T(8,128)(2,1)S(1)} %bitcast_convert_fusion), channel_id=1, source_target_pairs={{0,6},{2,4},{4,2},{6,0},{1,7},{3,5},{5,3},{7,1},{8,14},{10,12},{12... | collective-permute-start | bytes 393224 | tf_op jit(solution)/shard_map/ppermute | solution.py:25
  30.7 3.9 %collective-permute-start.2 = (bf16[128,512]{1,0:T(8,128)(2,1)S(1)}, bf16[128,512]{1,0:T(8,128)(2,1)S(1)}, u32[]{:S(2)}, u32[]{:S(2)}) collective-permute-start(bf16[128,512]{1,0:T(8,128)(2,1)S(1)} %bitcast_convert_fusion), channel_id=1, source_target_pairs={{0,4},{2,6},{4,0},{6,2},{1,5},{3,7},{5,1},{7,3},{8,12},{10,14},{12... | collective-permute-start | bytes 393224 | tf_op jit(solution)/shard_map/ppermute | solution.py:25
  34.6 0.0 collective-permute-done.1
  34.6 3.0 %collective-permute-start.4 = (bf16[128,512]{1,0:T(8,128)(2,1)S(1)}, bf16[128,512]{1,0:T(8,128)(2,1)S(1)}, u32[]{:S(2)}, u32[]{:S(2)}) collective-permute-start(bf16[128,512]{1,0:T(8,128)(2,1)S(1)} %bitcast_convert_fusion), channel_id=1, source_target_pairs={{0,32},{32,0},{64,96},{96,64},{128,160},{160,128},{192,224},{224,1... | collective-permute-start | bytes 393224 | tf_op jit(solution)/shard_map/ppermute | solution.py:25
  37.7 0.0 collective-permute-done.3
  37.7 6.1 %collective-permute-done.2 = bf16[128,512]{1,0:T(8,128)(2,1)S(1)} collective-permute-done((bf16[128,512]{1,0:T(8,128)(2,1)S(1)}, bf16[128,512]{1,0:T(8,128)(2,1)S(1)}, u32[]{:S(2)}, u32[]{:S(2)}) %collective-permute-start.2) | collective-permute-done | bytes 131104 | tf_op jit(solution)/shard_map/ppermute | solution.py:25
  43.8 0.0 collective-permute-done.4
  43.8 4.2 %collective-permute-start.8 = (bf16[128,512]{1,0:T(8,128)(2,1)S(1)}, bf16[128,512]{1,0:T(8,128)(2,1)S(1)}, u32[]{:S(2)}, u32[]{:S(2)}) collective-permute-start(bf16[128,512]{1,0:T(8,128)(2,1)S(1)} %convert_add_fusion.2), channel_id=1, source_target_pairs={{0,64},{32,96},{64,0},{96,32},{128,192},{160,224},{192,128},{224,1... | collective-permute-start | bytes 393224 | tf_op jit(solution)/shard_map/ppermute | solution.py:25
  48.0 4.4 %collective-permute-start.7 = (bf16[512,512]{1,0:T(8,128)(2,1)S(1)}, bf16[512,512]{1,0:T(8,128)(2,1)S(1)}, u32[]{:S(2)}, u32[]{:S(2)}) collective-permute-start(bf16[512,512]{1,0:T(8,128)(2,1)S(1)} %pad_maximum_fusion.refs_2_), channel_id=1, source_target_pairs={{0,24},{8,16},{16,8},{24,0},{1,25},{9,17},{17,9},{25,1},{2,26},{10... | collective-permute-start | bytes 1572872 | tf_op jit(solution)/shard_map/ppermute | solution.py:25
  52.4 2.5 %collective-permute-start.6 = (bf16[512,512]{1,0:T(8,128)(2,1)S(1)}, bf16[512,512]{1,0:T(8,128)(2,1)S(1)}, u32[]{:S(2)}, u32[]{:S(2)}) collective-permute-start(bf16[512,512]{1,0:T(8,128)(2,1)S(1)} %pad_maximum_fusion.refs_2_), channel_id=1, source_target_pairs={{0,16},{8,24},{16,0},{24,8},{1,17},{9,25},{17,1},{25,9},{2,18},{10... | collective-permute-start | bytes 1572872 | tf_op jit(solution)/shard_map/ppermute | solution.py:25
  54.9 2.1 %collective-permute-start.5 = (bf16[512,512]{1,0:T(8,128)(2,1)S(1)}, bf16[512,512]{1,0:T(8,128)(2,1)S(1)}, u32[]{:S(2)}, u32[]{:S(2)}) collective-permute-start(bf16[512,512]{1,0:T(8,128)(2,1)S(1)} %pad_maximum_fusion.refs_2_), channel_id=1, source_target_pairs={{0,8},{8,0},{16,24},{24,16},{1,9},{9,1},{17,25},{25,17},{2,10},{10... | collective-permute-start | bytes 1572872 | tf_op jit(solution)/shard_map/ppermute | solution.py:25
  57.0 0.0 collective-permute-done.8
  57.1 0.0 copy-start.7
  57.1 0.0 all-to-all-done
  57.1 5.6 %collective-permute-start.9 = (bf16[128,512]{1,0:T(8,128)(2,1)S(1)}, bf16[128,512]{1,0:T(8,128)(2,1)}, u32[]{:S(2)}, u32[]{:S(2)}) collective-permute-start(bf16[128,512]{1,0:T(8,128)(2,1)S(1)} %convert_add_fusion.1), channel_id=1, source_target_pairs={{0,128},{32,160},{64,192},{96,224},{128,0},{160,32},{192,64},{224,... | collective-permute-start | bytes 393224 | tf_op jit(solution)/shard_map/ppermute | solution.py:25
  62.8 2.8 %reduce_sum.21.refs_6_ = bf16[512,512]{1,0:T(8,128)(2,1)} reduce(bf16[4,512,512]{2,1,0:T(8,128)(2,1)} %all-to-all-done, bf16[]{:T(256)} %constant.9.clone.1), dimensions={0}, to_apply=%region_0.0 | reduce | flops 786432 | bytes 2621442 | tf_op jit(solution)/shard_map/reduce_sum | solution.py:38
  65.6 5.4 %all-to-all-start.1 = ((bf16[4,128,512]{2,1,0:T(8,128)(2,1)}), bf16[4,128,512]{2,1,0:T(8,128)(2,1)}, u32[]{:S(2)}, u32[]{:S(2)}) async-start(bf16[4,128,512]{2,1,0:T(8,128)(2,1)} %bitcast.5), calls=%async_computation.1 | async-start | bytes 1048576 | tf_op jit(solution)/shard_map/all_to_all | solution.py:34
  71.1 0.0 copy-done.7
  71.1 0.0 collective-permute-done.9
  71.1 1.0 %fusion.7 = (bf16[128,512]{1,0:T(8,128)(2,1)S(1)}, f32[128,512]{1,0:T(8,128)S(1)}) fusion(bf16[128,512]{1,0:T(8,128)(2,1)} %collective-permute-done.9, bf16[128,512]{1,0:T(8,128)(2,1)} %copy-done.7), kind=kLoop, calls=%fused_computation.25 | loop fusion | flops 262144 | bytes 655360 | tf_op jit(solution)/shard_map/convert_element_type | solution.py:29
  72.1 2.0 %collective-permute-done.7.refs_5_ = bf16[512,512]{1,0:T(8,128)(2,1)S(1)} collective-permute-done((bf16[512,512]{1,0:T(8,128)(2,1)S(1)}, bf16[512,512]{1,0:T(8,128)(2,1)S(1)}, u32[]{:S(2)}, u32[]{:S(2)}) %collective-permute-start.7) | collective-permute-done | bytes 524320 | tf_op jit(solution)/shard_map/ppermute | solution.py:25
  74.1 0.0 collective-permute-done.6.refs_4_
  74.1 2.3 %collective-permute-done.5.refs_3_ = bf16[512,512]{1,0:T(8,128)(2,1)S(1)} collective-permute-done((bf16[512,512]{1,0:T(8,128)(2,1)S(1)}, bf16[512,512]{1,0:T(8,128)(2,1)S(1)}, u32[]{:S(2)}, u32[]{:S(2)}) %collective-permute-start.5) | collective-permute-done | bytes 524320 | tf_op jit(solution)/shard_map/ppermute | solution.py:25
  76.4 0.0 copy-start.1
  76.4 1.2 %their_keys.1 = f32[256,512]{1,0:T(8,128)S(1)} custom-call(s32[3]{0:T(128)S(1)} %pad_add_fusion.refs_0_, bf16[256,2560]{1,0:T(8,128)(2,1)S(1)} %collective-permute-done.refs_3_.refs_1_, bf16[512,512]{1,0:T(8,128)(2,1)S(1)} %pad_maximum_fusion.refs_2_, bf16[512,512]{1,0:T(8,128)(2,1)S(1)} %collective-permute-done.5.refs_3_, ...), custom_call_target="tpu_custom_call" | custom-call | flops 536870912 | bytes 6815768 | tf_op jit(solution)/shard_map/their_keys/pallas_call | solution.py:48
  77.6 4.8 %collective-permute-start.10 = (f32[256,512]{1,0:T(8,128)S(1)}, f32[256,512]{1,0:T(8,128)S(1)}, u32[]{:S(2)}, u32[]{:S(2)}) collective-permute-start(f32[256,512]{1,0:T(8,128)S(1)} %their_keys.1), channel_id=1, source_target_pairs={{0,1},{1,0},{2,3},{3,2},{4,5},{5,4},{6,7},{7,6},{8,9},{9,8},{10,11... | collective-permute-start | bytes 1572872 | tf_op jit(solution)/shard_map/ppermute | solution.py:25
  82.4 0.0 copy-done.1
  82.4 1.3 %our_keys.1 = f32[256,512]{1,0:T(8,128)S(1)} custom-call(s32[3]{0:T(128)S(1)} %pad_add_fusion.refs_0_, bf16[256,4096]{1,0:T(8,128)(2,1)S(1)} %copy-done.1, bf16[512,512]{1,0:T(8,128)(2,1)S(1)} %pad_maximum_fusion.refs_2_, bf16[512,512]{1,0:T(8,128)(2,1)S(1)} %collective-permute-done.5.refs_3_, bf16[512,512]{1,0:T(8,128)(2,1)S(1)} %collective-permute-done.6.refs_4_, ...), custom_call_target="tpu_custom_call" | custom-call | flops 536870912 | bytes 8388632 | tf_op jit(solution)/shard_map/our_keys/pallas_call | solution.py:48
  83.7 0.0 copy-start.3
  83.7 0.0 copy-start.4
  83.7 0.0 copy-start.6
  83.7 0.0 copy-start.8
  83.8 0.0 copy-start.9
  83.8 2.1 %collective-permute-start.11 = (bf16[128,512]{1,0:T(8,128)(2,1)S(1)}, bf16[128,512]{1,0:T(8,128)(2,1)S(1)}, u32[]{:S(2)}, u32[]{:S(2)}) collective-permute-start(bf16[128,512]{1,0:T(8,128)(2,1)S(1)} %get-tuple-element.23), channel_id=1, source_target_pairs={{0,256},{256,0},{1,257},{257,1},{2,258},{258,2},{3,259},{259,3},{4... | collective-permute-start | bytes 393224 | tf_op jit(solution)/shard_map/ppermute | solution.py:25
  85.8 0.0 collective-permute-done.10
  85.8 0.8 multiply_convert_fusion
  86.7 0.0 all-to-all-done.1
  86.7 1.1 %convert_reduce_fusion = f32[128,512]{1,0:T(8,128)S(1)} fusion(bf16[4,128,512]{2,1,0:T(8,128)(2,1)} %all-to-all-done.1), kind=kLoop, calls=%fused_computation | loop fusion | flops 458752 | bytes 786432 | tf_op jit(solution)/shard_map/reduce_sum | solution.py:38
  87.8 0.0 copy-done.3
  87.8 0.0 copy-done.4
  87.8 0.9 bitcast_add_fusion
  88.7 2.2 %collective-permute-done.11 = bf16[128,512]{1,0:T(8,128)(2,1)S(1)} collective-permute-done((bf16[128,512]{1,0:T(8,128)(2,1)S(1)}, bf16[128,512]{1,0:T(8,128)(2,1)S(1)}, u32[]{:S(2)}, u32[]{:S(2)}) %collective-permute-start.11) | collective-permute-done | bytes 131104 | tf_op jit(solution)/shard_map/ppermute | solution.py:25
  90.9 0.0 copy-done.6
  90.9 0.0 copy-done.8
  90.9 0.0 copy-done.9
  90.9 1.0 %multiply_bitcast_fusion = (f32[1,128,512]{2,1,0:T(8,128)}, f32[128,512]{1,0:T(8,128)}, f32[128,512]{1,0:T(8,128)}) fusion(f32[1,128,512]{2,1,0:T(8,128)S(1)} %copy-done.6, f32[1,128,512]{2,1,0:T(8,128)S(1)} %copy-done.3, f32[128,512]{1,0:T(8,128)S(1)} %convert_reduce_fusion, f32[1,128,512]{2,1,0:T(8,128)S(1)} %copy-done.4, f32[128,512]{1,0:T(8,128)S(1)} %copy-done.8, ...), kind=kLoop, calls=%fused_computation.16 | loop fusion | flops 1769472 | bytes 2621440 | tf_op jit(solution)/shard_map/broadcast_in_dim | solution.py:165
  (4 shorter events, 0.1 us)
Async XLA Ops:
  0.7 1.6 %copy-start = (bf16[256,4096]{1,0:T(8,128)(2,1)S(1)}, bf16[256,4096]{1,0:T(8,128)(2,1)}, u32[]{:S(2)}) copy-start(bf16[256,4096]{1,0:T(8,128)(2,1)} %refs_1_.5) | copy-start | bytes 6291460
  2.3 0.9 %copy-start.2 = (bf16[256,512]{1,0:T(8,128)(2,1)S(1)}, bf16[256,512]{1,0:T(8,128)(2,1)}, u32[]{:S(2)}) copy-start(bf16[256,512]{1,0:T(8,128)(2,1)} %refs_2_.3) | copy-start | bytes 786436
  4.0 11.4 %collective-permute-start = (bf16[256,2560]{1,0:T(8,128)(2,1)S(1)}, bf16[256,2560]{1,0:T(8,128)(2,1)S(1)}, u32[]{:S(2)}, u32[]{:S(2)}) collective-permute-start(bf16[256,2560]{1,0:T(8,128)(2,1)S(1)} %send.1), channel_id=1, source_target_pairs={{0,1},{1,0},{2,3},{3,2},{4,5},{5,4},{6,7},{7,6},{8,9},{9,8},{10,11... | collective-permute-start | bytes 3932168 | tf_op jit(solution)/shard_map/ppermute | solution.py:25
  18.6 4.6 %copy-start.5 = (f32[1,128,512]{2,1,0:T(8,128)S(1)}, f32[1,128,512]{2,1,0:T(8,128)}, u32[]{:S(2)}) copy-start(f32[1,128,512]{2,1,0:T(8,128)} %param.9) | copy-start | bytes 786436
  18.6 38.5 %all-to-all-start = ((bf16[4,512,512]{2,1,0:T(8,128)(2,1)}), bf16[4,512,512]{2,1,0:T(8,128)(2,1)}, u32[]{:S(2)}, u32[]{:S(2)}) async-start(bf16[4,512,512]{2,1,0:T(8,128)(2,1)} %grad.1), calls=%async_computation | async-start | bytes 4194304 | tf_op jit(solution)/shard_map/all_to_all | solution.py:34
  23.2 11.4 %collective-permute-start.1 = (bf16[128,512]{1,0:T(8,128)(2,1)S(1)}, bf16[128,512]{1,0:T(8,128)(2,1)S(1)}, u32[]{:S(2)}, u32[]{:S(2)}) collective-permute-start(bf16[128,512]{1,0:T(8,128)(2,1)S(1)} %bitcast_convert_fusion), channel_id=1, source_target_pairs={{0,2},{2,0},{4,6},{6,4},{1,3},{3,1},{5,7},{7,5},{8,10},{10,8},{12,... | collective-permute-start | bytes 393224 | tf_op jit(solution)/shard_map/ppermute | solution.py:25
  25.1 12.5 %collective-permute-start.3 = (bf16[128,512]{1,0:T(8,128)(2,1)S(1)}, bf16[128,512]{1,0:T(8,128)(2,1)S(1)}, u32[]{:S(2)}, u32[]{:S(2)}) collective-permute-start(bf16[128,512]{1,0:T(8,128)(2,1)S(1)} %bitcast_convert_fusion), channel_id=1, source_target_pairs={{0,6},{2,4},{4,2},{6,0},{1,7},{3,5},{5,3},{7,1},{8,14},{10,12},{12... | collective-permute-start | bytes 393224 | tf_op jit(solution)/shard_map/ppermute | solution.py:25
  30.7 13.0 %collective-permute-start.2 = (bf16[128,512]{1,0:T(8,128)(2,1)S(1)}, bf16[128,512]{1,0:T(8,128)(2,1)S(1)}, u32[]{:S(2)}, u32[]{:S(2)}) collective-permute-start(bf16[128,512]{1,0:T(8,128)(2,1)S(1)} %bitcast_convert_fusion), channel_id=1, source_target_pairs={{0,4},{2,6},{4,0},{6,2},{1,5},{3,7},{5,1},{7,3},{8,12},{10,14},{12... | collective-permute-start | bytes 393224 | tf_op jit(solution)/shard_map/ppermute | solution.py:25
  34.6 9.1 %collective-permute-start.4 = (bf16[128,512]{1,0:T(8,128)(2,1)S(1)}, bf16[128,512]{1,0:T(8,128)(2,1)S(1)}, u32[]{:S(2)}, u32[]{:S(2)}) collective-permute-start(bf16[128,512]{1,0:T(8,128)(2,1)S(1)} %bitcast_convert_fusion), channel_id=1, source_target_pairs={{0,32},{32,0},{64,96},{96,64},{128,160},{160,128},{192,224},{224,1... | collective-permute-start | bytes 393224 | tf_op jit(solution)/shard_map/ppermute | solution.py:25
  43.8 13.2 %collective-permute-start.8 = (bf16[128,512]{1,0:T(8,128)(2,1)S(1)}, bf16[128,512]{1,0:T(8,128)(2,1)S(1)}, u32[]{:S(2)}, u32[]{:S(2)}) collective-permute-start(bf16[128,512]{1,0:T(8,128)(2,1)S(1)} %convert_add_fusion.2), channel_id=1, source_target_pairs={{0,64},{32,96},{64,0},{96,32},{128,192},{160,224},{192,128},{224,1... | collective-permute-start | bytes 393224 | tf_op jit(solution)/shard_map/ppermute | solution.py:25
  48.0 26.1 %collective-permute-start.7 = (bf16[512,512]{1,0:T(8,128)(2,1)S(1)}, bf16[512,512]{1,0:T(8,128)(2,1)S(1)}, u32[]{:S(2)}, u32[]{:S(2)}) collective-permute-start(bf16[512,512]{1,0:T(8,128)(2,1)S(1)} %pad_maximum_fusion.refs_2_), channel_id=1, source_target_pairs={{0,24},{8,16},{16,8},{24,0},{1,25},{9,17},{17,9},{25,1},{2,26},{10... | collective-permute-start | bytes 1572872 | tf_op jit(solution)/shard_map/ppermute | solution.py:25
  52.4 21.7 %collective-permute-start.6 = (bf16[512,512]{1,0:T(8,128)(2,1)S(1)}, bf16[512,512]{1,0:T(8,128)(2,1)S(1)}, u32[]{:S(2)}, u32[]{:S(2)}) collective-permute-start(bf16[512,512]{1,0:T(8,128)(2,1)S(1)} %pad_maximum_fusion.refs_2_), channel_id=1, source_target_pairs={{0,16},{8,24},{16,0},{24,8},{1,17},{9,25},{17,1},{25,9},{2,18},{10... | collective-permute-start | bytes 1572872 | tf_op jit(solution)/shard_map/ppermute | solution.py:25
  54.9 21.5 %collective-permute-start.5 = (bf16[512,512]{1,0:T(8,128)(2,1)S(1)}, bf16[512,512]{1,0:T(8,128)(2,1)S(1)}, u32[]{:S(2)}, u32[]{:S(2)}) collective-permute-start(bf16[512,512]{1,0:T(8,128)(2,1)S(1)} %pad_maximum_fusion.refs_2_), channel_id=1, source_target_pairs={{0,8},{8,0},{16,24},{24,16},{1,9},{9,1},{17,25},{25,17},{2,10},{10... | collective-permute-start | bytes 1572872 | tf_op jit(solution)/shard_map/ppermute | solution.py:25
  57.1 14.0 %copy-start.7 = (bf16[128,512]{1,0:T(8,128)(2,1)}, bf16[128,512]{1,0:T(8,128)(2,1)S(1)}, u32[]{:S(2)}) copy-start(bf16[128,512]{1,0:T(8,128)(2,1)S(1)} %convert_add_fusion.1) | copy-start | bytes 393220
  57.1 13.9 %collective-permute-start.9 = (bf16[128,512]{1,0:T(8,128)(2,1)S(1)}, bf16[128,512]{1,0:T(8,128)(2,1)}, u32[]{:S(2)}, u32[]{:S(2)}) collective-permute-start(bf16[128,512]{1,0:T(8,128)(2,1)S(1)} %convert_add_fusion.1), channel_id=1, source_target_pairs={{0,128},{32,160},{64,192},{96,224},{128,0},{160,32},{192,64},{224,... | collective-permute-start | bytes 393224 | tf_op jit(solution)/shard_map/ppermute | solution.py:25
  65.6 21.1 %all-to-all-start.1 = ((bf16[4,128,512]{2,1,0:T(8,128)(2,1)}), bf16[4,128,512]{2,1,0:T(8,128)(2,1)}, u32[]{:S(2)}, u32[]{:S(2)}) async-start(bf16[4,128,512]{2,1,0:T(8,128)(2,1)} %bitcast.5), calls=%async_computation.1 | async-start | bytes 1048576 | tf_op jit(solution)/shard_map/all_to_all | solution.py:34
  76.4 6.0 %copy-start.1 = (bf16[256,4096]{1,0:T(8,128)(2,1)S(1)}, bf16[256,4096]{1,0:T(8,128)(2,1)}, u32[]{:S(2)}) copy-start(bf16[256,4096]{1,0:T(8,128)(2,1)} %refs_1_.5) | copy-start | bytes 6291460
  77.6 8.2 %collective-permute-start.10 = (f32[256,512]{1,0:T(8,128)S(1)}, f32[256,512]{1,0:T(8,128)S(1)}, u32[]{:S(2)}, u32[]{:S(2)}) collective-permute-start(f32[256,512]{1,0:T(8,128)S(1)} %their_keys.1), channel_id=1, source_target_pairs={{0,1},{1,0},{2,3},{3,2},{4,5},{5,4},{6,7},{7,6},{8,9},{9,8},{10,11... | collective-permute-start | bytes 1572872 | tf_op jit(solution)/shard_map/ppermute | solution.py:25
  83.7 4.1 %copy-start.3 = (f32[1,128,512]{2,1,0:T(8,128)S(1)}, f32[1,128,512]{2,1,0:T(8,128)}, u32[]{:S(2)}) copy-start(f32[1,128,512]{2,1,0:T(8,128)} %param.11) | copy-start | bytes 786436
  83.7 4.1 %copy-start.4 = (f32[1,128,512]{2,1,0:T(8,128)S(1)}, f32[1,128,512]{2,1,0:T(8,128)}, u32[]{:S(2)}) copy-start(f32[1,128,512]{2,1,0:T(8,128)} %param.10) | copy-start | bytes 786436
  83.7 7.2 %copy-start.6 = (f32[1,128,512]{2,1,0:T(8,128)S(1)}, f32[1,128,512]{2,1,0:T(8,128)}, u32[]{:S(2)}) copy-start(f32[1,128,512]{2,1,0:T(8,128)} %param.9) | copy-start | bytes 786436
  83.7 7.2 %copy-start.8 = (f32[128,512]{1,0:T(8,128)S(1)}, f32[128,512]{1,0:T(8,128)}, u32[]{:S(2)}) copy-start(f32[128,512]{1,0:T(8,128)} %param.12) | copy-start | bytes 786436
  83.8 7.2 %copy-start.9 = (f32[128,512]{1,0:T(8,128)S(1)}, f32[128,512]{1,0:T(8,128)}, u32[]{:S(2)}) copy-start(f32[128,512]{1,0:T(8,128)} %param.13) | copy-start | bytes 786436
  83.8 7.2 %collective-permute-start.11 = (bf16[128,512]{1,0:T(8,128)(2,1)S(1)}, bf16[128,512]{1,0:T(8,128)(2,1)S(1)}, u32[]{:S(2)}, u32[]{:S(2)}) collective-permute-start(bf16[128,512]{1,0:T(8,128)(2,1)S(1)} %get-tuple-element.23), channel_id=1, source_target_pairs={{0,256},{256,0},{1,257},{257,1},{2,258},{258,2},{3,259},{259,3},{4... | collective-permute-start | bytes 393224 | tf_op jit(solution)/shard_map/ppermute | solution.py:25

commit v4 on v3

--- a/solution.py
+++ b/solution.py
@@ -130,11 +130,13 @@
 
     late_half = lax.optimization_barrier((weight_half, term))[0]
     near = [late_half] + [trade(late_half, "zh", k) for k in (1, 2, 3)]
-    pair = add_other(lax.optimization_barrier((late_half, near[1]))[0], "y", 1)
+    own = lax.optimization_barrier((late_half, near[1]))[0]
+    others = [trade(own, "y", mask) for mask in (1, 2, 3)]
     column = jnp.concatenate(near, axis=0)
-    column, pair = lax.optimization_barrier((column, pair))
+    column, others[0] = lax.optimization_barrier((column, others[0]))
     halves = [column] + [trade(column, "x", j) for j in (1, 2, 3)]
-    four = add_other(pair, "y", 2)
+    wide = [value.astype(F32) for value in (own, *others)]
+    four = (wide[0] + wide[1]) + (wide[2] + wide[3])
     come, four = lax.optimization_barrier((come, four))
     part = total(come).astype(BF16)
     eight = add_other(four, "y", 4)

time: 92.7 us -> 88.6 us (0.956)
  waiting for transfers between devices: 15.2 us -> 6.86 us
  starting transfers between devices: 58.9 us -> 63.1 us
    ppermute x12 -> x13, waiting for transfers between devices: 15.2 us -> 6.85 us  [trade(): lax.ppermute(block, axis, [(i, i ^ mask) for i in range(lax.axis_size(axi...]
    ppermute x12 -> x13, starting transfers between devices: 48.8 us -> 53.1 us  [trade(): lax.ppermute(block, axis, [(i, i ^ mask) for i in range(lax.axis_size(axi...]
  transfers between devices with their start and end apart: 14 -> 15, of which waited for: 5 -> 5; matrix products, arithmetic and copies ran while one was open for 7% -> 8% of each run, Pallas kernels for 3% -> 3%
where the time goes in v4:
time: 88.6 us; the launch traced here: 87.9 us
  starting transfers between devices  63.1 us (71%)
  other arithmetic  7.93 us (9%)
  waiting for transfers between devices  6.86 us (8%)
  Pallas kernels  6.41 us (7%)
  local copies, waits for them, and re-layouts  2.59 us (3%)
  between operations  0.95 us (1%)
    ppermute x13, starting transfers between devices, trade(): lax.ppermute(block, axis, [(i, i ^ mask) for i in range(lax.axis_size(axi...  53.1 us
    all_to_all x2, starting transfers between devices, exchange(): return lax.all_to_all(blocks, axis, 0, 0, tiled=True)  10 us
    ppermute x13, waiting for transfers between devices, trade(): lax.ppermute(block, axis, [(i, i ^ mask) for i in range(lax.axis_size(axi...  6.85 us
    pallas_call x4, Pallas kernels, call(): pl.pallas_call(body, in_specs=[SMEM] + [VMEM] * (count - 1) + [pl.BlockSp...  6.41 us
    reduce_sum x2, other arithmetic, total(): return jnp.sum(blocks.astype(F32), axis=0)  4 us
    unnamed x20, local copies, waits for them, and re-layouts  2.59 us
  transfers between devices with their start and end apart: 15, of which 5 were waited for; matrix products, arithmetic and copies ran while one was open for 8% of the time, Pallas kernels for 3%

profile of v4, /device:TPU:1, one launch (start us, length us, event | category | flops | bytes accessed | tf_op | source)
XLA Modules:
  0.0 87.9 jit_solution(8787802638600670863)
XLA Ops:
  0.6 0.1 pad_add_fusion.refs_0_
  0.7 0.0 copy-start
  0.7 1.6 %copy-done = bf16[256,4096]{1,0:T(8,128)(2,1)S(1)} copy-done((bf16[256,4096]{1,0:T(8,128)(2,1)S(1)}, bf16[256,4096]{1,0:T(8,128)(2,1)}, u32[]{:S(2)}) %copy-start) | copy-done | bytes 2097176
  2.3 0.0 copy-start.2
  2.3 0.9 %copy-done.2 = bf16[256,512]{1,0:T(8,128)(2,1)S(1)} copy-done((bf16[256,512]{1,0:T(8,128)(2,1)S(1)}, bf16[256,512]{1,0:T(8,128)(2,1)}, u32[]{:S(2)}) %copy-start.2) | copy-done | bytes 262168
  3.3 0.8 send.1
  4.0 8.8 %collective-permute-start = (bf16[256,2560]{1,0:T(8,128)(2,1)S(1)}, bf16[256,2560]{1,0:T(8,128)(2,1)S(1)}, u32[]{:S(2)}, u32[]{:S(2)}) collective-permute-start(bf16[256,2560]{1,0:T(8,128)(2,1)S(1)} %send.1), channel_id=1, source_target_pairs={{0,1},{1,0},{2,3},{3,2},{4,5},{5,4},{6,7},{7,6},{8,9},{9,8},{10,11... | collective-permute-start | bytes 3932168 | tf_op jit(solution)/shard_map/ppermute | solution.py:25
  12.8 2.6 %collective-permute-done.refs_3_.refs_1_ = bf16[256,2560]{1,0:T(8,128)(2,1)S(1)} collective-permute-done((bf16[256,2560]{1,0:T(8,128)(2,1)S(1)}, bf16[256,2560]{1,0:T(8,128)(2,1)S(1)}, u32[]{:S(2)}, u32[]{:S(2)}) %collective-permute-start) | collective-permute-done | bytes 1310752 | tf_op jit(solution)/shard_map/ppermute | solution.py:25
  15.5 3.1 %grad.1 = bf16[4,512,512]{2,1,0:T(8,128)(2,1)} custom-call(s32[3]{0:T(128)S(1)} %pad_add_fusion.refs_0_, bf16[256,4096]{1,0:T(8,128)(2,1)S(1)} %copy-done, bf16[256,512]{1,0:T(8,128)(2,1)S(1)} %copy-done.2, bf16[256,2560]{1,0:T(8,128)(2,1)S(1)} %collective-permute-done.refs_3_.refs_1_), custom_call_target="tpu_custom_call" | custom-call | flops 1073741824 | bytes 7340056 | tf_op jit(solution)/shard_map/grad/pallas_call | solution.py:48
  18.6 0.0 copy-start.5
  18.6 4.6 %all-to-all-start = ((bf16[4,512,512]{2,1,0:T(8,128)(2,1)}), bf16[4,512,512]{2,1,0:T(8,128)(2,1)}, u32[]{:S(2)}, u32[]{:S(2)}) async-start(bf16[4,512,512]{2,1,0:T(8,128)(2,1)} %grad.1), calls=%async_computation | async-start | bytes 4194304 | tf_op jit(solution)/shard_map/all_to_all | solution.py:34
  23.2 0.0 copy-done.5
  23.2 1.9 %collective-permute-start.1 = (bf16[128,512]{1,0:T(8,128)(2,1)S(1)}, bf16[128,512]{1,0:T(8,128)(2,1)S(1)}, u32[]{:S(2)}, u32[]{:S(2)}) collective-permute-start(bf16[128,512]{1,0:T(8,128)(2,1)S(1)} %bitcast_convert_fusion), channel_id=1, source_target_pairs={{0,2},{2,0},{4,6},{6,4},{1,3},{3,1},{5,7},{7,5},{8,10},{10,8},{12,... | collective-permute-start | bytes 393224 | tf_op jit(solution)/shard_map/ppermute | solution.py:25
  25.2 5.5 %collective-permute-start.3 = (bf16[128,512]{1,0:T(8,128)(2,1)S(1)}, bf16[128,512]{1,0:T(8,128)(2,1)S(1)}, u32[]{:S(2)}, u32[]{:S(2)}) collective-permute-start(bf16[128,512]{1,0:T(8,128)(2,1)S(1)} %bitcast_convert_fusion), channel_id=1, source_target_pairs={{0,6},{2,4},{4,2},{6,0},{1,7},{3,5},{5,3},{7,1},{8,14},{10,12},{12... | collective-permute-start | bytes 393224 | tf_op jit(solution)/shard_map/ppermute | solution.py:25
  30.7 3.9 %collective-permute-start.2 = (bf16[128,512]{1,0:T(8,128)(2,1)S(1)}, bf16[128,512]{1,0:T(8,128)(2,1)S(1)}, u32[]{:S(2)}, u32[]{:S(2)}) collective-permute-start(bf16[128,512]{1,0:T(8,128)(2,1)S(1)} %bitcast_convert_fusion), channel_id=1, source_target_pairs={{0,4},{2,6},{4,0},{6,2},{1,5},{3,7},{5,1},{7,3},{8,12},{10,14},{12... | collective-permute-start | bytes 393224 | tf_op jit(solution)/shard_map/ppermute | solution.py:25
  34.6 0.0 collective-permute-done.1
  34.7 3.0 %collective-permute-start.4 = (bf16[128,512]{1,0:T(8,128)(2,1)S(1)}, bf16[128,512]{1,0:T(8,128)(2,1)S(1)}, u32[]{:S(2)}, u32[]{:S(2)}) collective-permute-start(bf16[128,512]{1,0:T(8,128)(2,1)S(1)} %bitcast_convert_fusion), channel_id=1, source_target_pairs={{0,32},{32,0},{64,96},{96,64},{128,160},{160,128},{192,224},{224,1... | collective-permute-start | bytes 393224 | tf_op jit(solution)/shard_map/ppermute | solution.py:25
  37.7 4.1 %collective-permute-start.9 = (bf16[128,512]{1,0:T(8,128)(2,1)S(1)}, bf16[128,512]{1,0:T(8,128)(2,1)S(1)}, u32[]{:S(2)}, u32[]{:S(2)}) collective-permute-start(bf16[128,512]{1,0:T(8,128)(2,1)S(1)} %bitcast_convert_fusion), channel_id=1, source_target_pairs={{0,96},{32,64},{64,32},{96,0},{128,224},{160,192},{192,160},{224,1... | collective-permute-start | bytes 393224 | tf_op jit(solution)/shard_map/ppermute | solution.py:25
  41.8 2.0 %collective-permute-start.8 = (bf16[128,512]{1,0:T(8,128)(2,1)S(1)}, bf16[128,512]{1,0:T(8,128)(2,1)S(1)}, u32[]{:S(2)}, u32[]{:S(2)}) collective-permute-start(bf16[128,512]{1,0:T(8,128)(2,1)S(1)} %bitcast_convert_fusion), channel_id=1, source_target_pairs={{0,64},{32,96},{64,0},{96,32},{128,192},{160,224},{192,128},{224,1... | collective-permute-start | bytes 393224 | tf_op jit(solution)/shard_map/ppermute | solution.py:25
  43.8 0.0 collective-permute-done.3
  43.8 0.0 collective-permute-done.2
  43.9 0.0 collective-permute-done.4
  43.9 4.5 %collective-permute-start.7 = (bf16[512,512]{1,0:T(8,128)(2,1)S(1)}, bf16[512,512]{1,0:T(8,128)(2,1)S(1)}, u32[]{:S(2)}, u32[]{:S(2)}) collective-permute-start(bf16[512,512]{1,0:T(8,128)(2,1)S(1)} %pad_maximum_fusion.refs_2_), channel_id=1, source_target_pairs={{0,24},{8,16},{16,8},{24,0},{1,25},{9,17},{17,9},{25,1},{2,26},{10... | collective-permute-start | bytes 1572872 | tf_op jit(solution)/shard_map/ppermute | solution.py:25
  48.4 2.5 %collective-permute-start.6 = (bf16[512,512]{1,0:T(8,128)(2,1)S(1)}, bf16[512,512]{1,0:T(8,128)(2,1)S(1)}, u32[]{:S(2)}, u32[]{:S(2)}) collective-permute-start(bf16[512,512]{1,0:T(8,128)(2,1)S(1)} %pad_maximum_fusion.refs_2_), channel_id=1, source_target_pairs={{0,16},{8,24},{16,0},{24,8},{1,17},{9,25},{17,1},{25,9},{2,18},{10... | collective-permute-start | bytes 1572872 | tf_op jit(solution)/shard_map/ppermute | solution.py:25
  50.9 2.0 %collective-permute-start.5 = (bf16[512,512]{1,0:T(8,128)(2,1)S(1)}, bf16[512,512]{1,0:T(8,128)(2,1)S(1)}, u32[]{:S(2)}, u32[]{:S(2)}) collective-permute-start(bf16[512,512]{1,0:T(8,128)(2,1)S(1)} %pad_maximum_fusion.refs_2_), channel_id=1, source_target_pairs={{0,8},{8,0},{16,24},{24,16},{1,9},{9,1},{17,25},{25,17},{2,10},{10... | collective-permute-start | bytes 1572872 | tf_op jit(solution)/shard_map/ppermute | solution.py:25
  52.9 0.0 collective-permute-done.9
  52.9 0.4 collective-permute-done.8
  53.3 0.1 add_add_fusion
  53.3 0.0 copy-start.7
  53.4 0.0 all-to-all-done
  53.4 7.0 %collective-permute-start.10 = (bf16[128,512]{1,0:T(8,128)(2,1)S(1)}, bf16[128,512]{1,0:T(8,128)(2,1)}, u32[]{:S(2)}, u32[]{:S(2)}) collective-permute-start(bf16[128,512]{1,0:T(8,128)(2,1)S(1)} %add_add_fusion), channel_id=1, source_target_pairs={{0,128},{32,160},{64,192},{96,224},{128,0},{160,32},{192,64},{224,... | collective-permute-start | bytes 393224 | tf_op jit(solution)/shard_map/ppermute | solution.py:25
  60.4 2.9 %reduce_sum.21.refs_6_ = bf16[512,512]{1,0:T(8,128)(2,1)} reduce(bf16[4,512,512]{2,1,0:T(8,128)(2,1)} %all-to-all-done, bf16[]{:T(256)} %constant.9.clone.1), dimensions={0}, to_apply=%region_0.0 | reduce | flops 786432 | bytes 2621442 | tf_op jit(solution)/shard_map/reduce_sum | solution.py:38
  63.2 5.4 %all-to-all-start.1 = ((bf16[4,128,512]{2,1,0:T(8,128)(2,1)}), bf16[4,128,512]{2,1,0:T(8,128)(2,1)}, u32[]{:S(2)}, u32[]{:S(2)}) async-start(bf16[4,128,512]{2,1,0:T(8,128)(2,1)} %bitcast.5), calls=%async_computation.1 | async-start | bytes 1048576 | tf_op jit(solution)/shard_map/all_to_all | solution.py:34
  68.7 0.0 copy-done.7
  68.7 0.0 collective-permute-done.10
  68.7 1.0 %fusion.7 = (bf16[128,512]{1,0:T(8,128)(2,1)S(1)}, f32[128,512]{1,0:T(8,128)S(1)}) fusion(bf16[128,512]{1,0:T(8,128)(2,1)} %collective-permute-done.10, bf16[128,512]{1,0:T(8,128)(2,1)} %copy-done.7), kind=kLoop, calls=%fused_computation.24 | loop fusion | flops 262144 | bytes 655360 | tf_op jit(solution)/shard_map/convert_element_type | solution.py:29
  69.7 1.1 %collective-permute-done.7.refs_5_ = bf16[512,512]{1,0:T(8,128)(2,1)S(1)} collective-permute-done((bf16[512,512]{1,0:T(8,128)(2,1)S(1)}, bf16[512,512]{1,0:T(8,128)(2,1)S(1)}, u32[]{:S(2)}, u32[]{:S(2)}) %collective-permute-start.7) | collective-permute-done | bytes 524320 | tf_op jit(solution)/shard_map/ppermute | solution.py:25
  70.8 0.0 collective-permute-done.6.refs_4_
  70.8 1.7 %collective-permute-done.5.refs_3_ = bf16[512,512]{1,0:T(8,128)(2,1)S(1)} collective-permute-done((bf16[512,512]{1,0:T(8,128)(2,1)S(1)}, bf16[512,512]{1,0:T(8,128)(2,1)S(1)}, u32[]{:S(2)}, u32[]{:S(2)}) %collective-permute-start.5) | collective-permute-done | bytes 524320 | tf_op jit(solution)/shard_map/ppermute | solution.py:25
  72.5 0.0 copy-start.1
  72.5 1.2 %their_keys.1 = f32[256,512]{1,0:T(8,128)S(1)} custom-call(s32[3]{0:T(128)S(1)} %pad_add_fusion.refs_0_, bf16[256,2560]{1,0:T(8,128)(2,1)S(1)} %collective-permute-done.refs_3_.refs_1_, bf16[512,512]{1,0:T(8,128)(2,1)S(1)} %pad_maximum_fusion.refs_2_, bf16[512,512]{1,0:T(8,128)(2,1)S(1)} %collective-permute-done.5.refs_3_, ...), custom_call_target="tpu_custom_call" | custom-call | flops 536870912 | bytes 6815768 | tf_op jit(solution)/shard_map/their_keys/pallas_call | solution.py:48
  73.7 4.6 %collective-permute-start.11 = (f32[256,512]{1,0:T(8,128)S(1)}, f32[256,512]{1,0:T(8,128)S(1)}, u32[]{:S(2)}, u32[]{:S(2)}) collective-permute-start(f32[256,512]{1,0:T(8,128)S(1)} %their_keys.1), channel_id=1, source_target_pairs={{0,1},{1,0},{2,3},{3,2},{4,5},{5,4},{6,7},{7,6},{8,9},{9,8},{10,11... | collective-permute-start | bytes 1572872 | tf_op jit(solution)/shard_map/ppermute | solution.py:25
  78.3 0.0 copy-done.1
  78.3 1.3 %our_keys.1 = f32[256,512]{1,0:T(8,128)S(1)} custom-call(s32[3]{0:T(128)S(1)} %pad_add_fusion.refs_0_, bf16[256,4096]{1,0:T(8,128)(2,1)S(1)} %copy-done.1, bf16[512,512]{1,0:T(8,128)(2,1)S(1)} %pad_maximum_fusion.refs_2_, bf16[512,512]{1,0:T(8,128)(2,1)S(1)} %collective-permute-done.5.refs_3_, bf16[512,512]{1,0:T(8,128)(2,1)S(1)} %collective-permute-done.6.refs_4_, ...), custom_call_target="tpu_custom_call" | custom-call | flops 536870912 | bytes 8388632 | tf_op jit(solution)/shard_map/our_keys/pallas_call | solution.py:48
  79.6 0.0 copy-start.3
  79.6 0.0 copy-start.4
  79.6 0.0 copy-start.6
  79.6 0.0 copy-start.8
  79.6 0.0 copy-start.9
  79.6 3.2 %collective-permute-start.12 = (bf16[128,512]{1,0:T(8,128)(2,1)S(1)}, bf16[128,512]{1,0:T(8,128)(2,1)S(1)}, u32[]{:S(2)}, u32[]{:S(2)}) collective-permute-start(bf16[128,512]{1,0:T(8,128)(2,1)S(1)} %get-tuple-element.23), channel_id=1, source_target_pairs={{0,256},{256,0},{1,257},{257,1},{2,258},{258,2},{3,259},{259,3},{4... | collective-permute-start | bytes 393224 | tf_op jit(solution)/shard_map/ppermute | solution.py:25
  82.9 0.0 collective-permute-done.11
  82.9 0.8 multiply_convert_fusion
  83.7 0.0 all-to-all-done.1
  83.7 1.1 %convert_reduce_fusion = f32[128,512]{1,0:T(8,128)S(1)} fusion(bf16[4,128,512]{2,1,0:T(8,128)(2,1)} %all-to-all-done.1), kind=kLoop, calls=%fused_computation | loop fusion | flops 458752 | bytes 786432 | tf_op jit(solution)/shard_map/reduce_sum | solution.py:38
  84.9 0.0 copy-done.3
  84.9 0.0 copy-done.4
  84.9 0.9 %bitcast_add_fusion = (f32[1,128,512]{2,1,0:T(8,128)}, f32[1,128,512]{2,1,0:T(8,128)}) fusion(f32[1,128,512]{2,1,0:T(8,128)S(1)} %copy-done.3, f32[128,512]{1,0:T(8,128)S(1)} %convert_reduce_fusion, f32[1,128,512]{2,1,0:T(8,128)S(1)} %copy-done.4), kind=kLoop, calls=%fused_computation.3 | loop fusion | flops 524288 | bytes 1310720 | tf_op jit(solution)/shard_map/add | solution.py:163
  85.8 1.1 %collective-permute-done.12 = bf16[128,512]{1,0:T(8,128)(2,1)S(1)} collective-permute-done((bf16[128,512]{1,0:T(8,128)(2,1)S(1)}, bf16[128,512]{1,0:T(8,128)(2,1)S(1)}, u32[]{:S(2)}, u32[]{:S(2)}) %collective-permute-start.12) | collective-permute-done | bytes 131104 | tf_op jit(solution)/shard_map/ppermute | solution.py:25
  86.8 0.0 copy-done.6
  86.8 0.0 copy-done.8
  86.8 0.0 copy-done.9
  86.8 1.0 %multiply_bitcast_fusion = (f32[1,128,512]{2,1,0:T(8,128)}, f32[128,512]{1,0:T(8,128)}, f32[128,512]{1,0:T(8,128)}) fusion(f32[1,128,512]{2,1,0:T(8,128)S(1)} %copy-done.6, f32[1,128,512]{2,1,0:T(8,128)S(1)} %copy-done.3, f32[128,512]{1,0:T(8,128)S(1)} %convert_reduce_fusion, f32[1,128,512]{2,1,0:T(8,128)S(1)} %copy-done.4, f32[128,512]{1,0:T(8,128)S(1)} %copy-done.8, ...), kind=kLoop, calls=%fused_computation.16 | loop fusion | flops 1769472 | bytes 2621440 | tf_op jit(solution)/shard_map/broadcast_in_dim | solution.py:167
  (2 shorter events, 0.1 us)
Async XLA Ops:
  0.7 1.6 %copy-start = (bf16[256,4096]{1,0:T(8,128)(2,1)S(1)}, bf16[256,4096]{1,0:T(8,128)(2,1)}, u32[]{:S(2)}) copy-start(bf16[256,4096]{1,0:T(8,128)(2,1)} %refs_1_.5) | copy-start | bytes 6291460
  2.3 0.9 %copy-start.2 = (bf16[256,512]{1,0:T(8,128)(2,1)S(1)}, bf16[256,512]{1,0:T(8,128)(2,1)}, u32[]{:S(2)}) copy-start(bf16[256,512]{1,0:T(8,128)(2,1)} %refs_2_.3) | copy-start | bytes 786436
  4.0 11.4 %collective-permute-start = (bf16[256,2560]{1,0:T(8,128)(2,1)S(1)}, bf16[256,2560]{1,0:T(8,128)(2,1)S(1)}, u32[]{:S(2)}, u32[]{:S(2)}) collective-permute-start(bf16[256,2560]{1,0:T(8,128)(2,1)S(1)} %send.1), channel_id=1, source_target_pairs={{0,1},{1,0},{2,3},{3,2},{4,5},{5,4},{6,7},{7,6},{8,9},{9,8},{10,11... | collective-permute-start | bytes 3932168 | tf_op jit(solution)/shard_map/ppermute | solution.py:25
  18.6 4.6 %copy-start.5 = (f32[1,128,512]{2,1,0:T(8,128)S(1)}, f32[1,128,512]{2,1,0:T(8,128)}, u32[]{:S(2)}) copy-start(f32[1,128,512]{2,1,0:T(8,128)} %param.9) | copy-start | bytes 786436
  18.6 34.8 %all-to-all-start = ((bf16[4,512,512]{2,1,0:T(8,128)(2,1)}), bf16[4,512,512]{2,1,0:T(8,128)(2,1)}, u32[]{:S(2)}, u32[]{:S(2)}) async-start(bf16[4,512,512]{2,1,0:T(8,128)(2,1)} %grad.1), calls=%async_computation | async-start | bytes 4194304 | tf_op jit(solution)/shard_map/all_to_all | solution.py:34
  23.2 11.4 %collective-permute-start.1 = (bf16[128,512]{1,0:T(8,128)(2,1)S(1)}, bf16[128,512]{1,0:T(8,128)(2,1)S(1)}, u32[]{:S(2)}, u32[]{:S(2)}) collective-permute-start(bf16[128,512]{1,0:T(8,128)(2,1)S(1)} %bitcast_convert_fusion), channel_id=1, source_target_pairs={{0,2},{2,0},{4,6},{6,4},{1,3},{3,1},{5,7},{7,5},{8,10},{10,8},{12,... | collective-permute-start | bytes 393224 | tf_op jit(solution)/shard_map/ppermute | solution.py:25
  25.2 18.7 %collective-permute-start.3 = (bf16[128,512]{1,0:T(8,128)(2,1)S(1)}, bf16[128,512]{1,0:T(8,128)(2,1)S(1)}, u32[]{:S(2)}, u32[]{:S(2)}) collective-permute-start(bf16[128,512]{1,0:T(8,128)(2,1)S(1)} %bitcast_convert_fusion), channel_id=1, source_target_pairs={{0,6},{2,4},{4,2},{6,0},{1,7},{3,5},{5,3},{7,1},{8,14},{10,12},{12... | collective-permute-start | bytes 393224 | tf_op jit(solution)/shard_map/ppermute | solution.py:25
  30.7 13.1 %collective-permute-start.2 = (bf16[128,512]{1,0:T(8,128)(2,1)S(1)}, bf16[128,512]{1,0:T(8,128)(2,1)S(1)}, u32[]{:S(2)}, u32[]{:S(2)}) collective-permute-start(bf16[128,512]{1,0:T(8,128)(2,1)S(1)} %bitcast_convert_fusion), channel_id=1, source_target_pairs={{0,4},{2,6},{4,0},{6,2},{1,5},{3,7},{5,1},{7,3},{8,12},{10,14},{12... | collective-permute-start | bytes 393224 | tf_op jit(solution)/shard_map/ppermute | solution.py:25
  34.7 9.2 %collective-permute-start.4 = (bf16[128,512]{1,0:T(8,128)(2,1)S(1)}, bf16[128,512]{1,0:T(8,128)(2,1)S(1)}, u32[]{:S(2)}, u32[]{:S(2)}) collective-permute-start(bf16[128,512]{1,0:T(8,128)(2,1)S(1)} %bitcast_convert_fusion), channel_id=1, source_target_pairs={{0,32},{32,0},{64,96},{96,64},{128,160},{160,128},{192,224},{224,1... | collective-permute-start | bytes 393224 | tf_op jit(solution)/shard_map/ppermute | solution.py:25
  37.7 15.2 %collective-permute-start.9 = (bf16[128,512]{1,0:T(8,128)(2,1)S(1)}, bf16[128,512]{1,0:T(8,128)(2,1)S(1)}, u32[]{:S(2)}, u32[]{:S(2)}) collective-permute-start(bf16[128,512]{1,0:T(8,128)(2,1)S(1)} %bitcast_convert_fusion), channel_id=1, source_target_pairs={{0,96},{32,64},{64,32},{96,0},{128,224},{160,192},{192,160},{224,1... | collective-permute-start | bytes 393224 | tf_op jit(solution)/shard_map/ppermute | solution.py:25
  41.8 11.5 %collective-permute-start.8 = (bf16[128,512]{1,0:T(8,128)(2,1)S(1)}, bf16[128,512]{1,0:T(8,128)(2,1)S(1)}, u32[]{:S(2)}, u32[]{:S(2)}) collective-permute-start(bf16[128,512]{1,0:T(8,128)(2,1)S(1)} %bitcast_convert_fusion), channel_id=1, source_target_pairs={{0,64},{32,96},{64,0},{96,32},{128,192},{160,224},{192,128},{224,1... | collective-permute-start | bytes 393224 | tf_op jit(solution)/shard_map/ppermute | solution.py:25
  43.9 26.9 %collective-permute-start.7 = (bf16[512,512]{1,0:T(8,128)(2,1)S(1)}, bf16[512,512]{1,0:T(8,128)(2,1)S(1)}, u32[]{:S(2)}, u32[]{:S(2)}) collective-permute-start(bf16[512,512]{1,0:T(8,128)(2,1)S(1)} %pad_maximum_fusion.refs_2_), channel_id=1, source_target_pairs={{0,24},{8,16},{16,8},{24,0},{1,25},{9,17},{17,9},{25,1},{2,26},{10... | collective-permute-start | bytes 1572872 | tf_op jit(solution)/shard_map/ppermute | solution.py:25
  48.4 22.4 %collective-permute-start.6 = (bf16[512,512]{1,0:T(8,128)(2,1)S(1)}, bf16[512,512]{1,0:T(8,128)(2,1)S(1)}, u32[]{:S(2)}, u32[]{:S(2)}) collective-permute-start(bf16[512,512]{1,0:T(8,128)(2,1)S(1)} %pad_maximum_fusion.refs_2_), channel_id=1, source_target_pairs={{0,16},{8,24},{16,0},{24,8},{1,17},{9,25},{17,1},{25,9},{2,18},{10... | collective-permute-start | bytes 1572872 | tf_op jit(solution)/shard_map/ppermute | solution.py:25
  50.9 21.5 %collective-permute-start.5 = (bf16[512,512]{1,0:T(8,128)(2,1)S(1)}, bf16[512,512]{1,0:T(8,128)(2,1)S(1)}, u32[]{:S(2)}, u32[]{:S(2)}) collective-permute-start(bf16[512,512]{1,0:T(8,128)(2,1)S(1)} %pad_maximum_fusion.refs_2_), channel_id=1, source_target_pairs={{0,8},{8,0},{16,24},{24,16},{1,9},{9,1},{17,25},{25,17},{2,10},{10... | collective-permute-start | bytes 1572872 | tf_op jit(solution)/shard_map/ppermute | solution.py:25
  53.3 15.3 %copy-start.7 = (bf16[128,512]{1,0:T(8,128)(2,1)}, bf16[128,512]{1,0:T(8,128)(2,1)S(1)}, u32[]{:S(2)}) copy-start(bf16[128,512]{1,0:T(8,128)(2,1)S(1)} %add_add_fusion) | copy-start | bytes 393220
  53.4 15.3 %collective-permute-start.10 = (bf16[128,512]{1,0:T(8,128)(2,1)S(1)}, bf16[128,512]{1,0:T(8,128)(2,1)}, u32[]{:S(2)}, u32[]{:S(2)}) collective-permute-start(bf16[128,512]{1,0:T(8,128)(2,1)S(1)} %add_add_fusion), channel_id=1, source_target_pairs={{0,128},{32,160},{64,192},{96,224},{128,0},{160,32},{192,64},{224,... | collective-permute-start | bytes 393224 | tf_op jit(solution)/shard_map/ppermute | solution.py:25
  63.2 20.5 %all-to-all-start.1 = ((bf16[4,128,512]{2,1,0:T(8,128)(2,1)}), bf16[4,128,512]{2,1,0:T(8,128)(2,1)}, u32[]{:S(2)}, u32[]{:S(2)}) async-start(bf16[4,128,512]{2,1,0:T(8,128)(2,1)} %bitcast.5), calls=%async_computation.1 | async-start | bytes 1048576 | tf_op jit(solution)/shard_map/all_to_all | solution.py:34
  72.5 5.8 %copy-start.1 = (bf16[256,4096]{1,0:T(8,128)(2,1)S(1)}, bf16[256,4096]{1,0:T(8,128)(2,1)}, u32[]{:S(2)}) copy-start(bf16[256,4096]{1,0:T(8,128)(2,1)} %refs_1_.5) | copy-start | bytes 6291460
  73.7 9.2 %collective-permute-start.11 = (f32[256,512]{1,0:T(8,128)S(1)}, f32[256,512]{1,0:T(8,128)S(1)}, u32[]{:S(2)}, u32[]{:S(2)}) collective-permute-start(f32[256,512]{1,0:T(8,128)S(1)} %their_keys.1), channel_id=1, source_target_pairs={{0,1},{1,0},{2,3},{3,2},{4,5},{5,4},{6,7},{7,6},{8,9},{9,8},{10,11... | collective-permute-start | bytes 1572872 | tf_op jit(solution)/shard_map/ppermute | solution.py:25
  79.6 5.3 %copy-start.3 = (f32[1,128,512]{2,1,0:T(8,128)S(1)}, f32[1,128,512]{2,1,0:T(8,128)}, u32[]{:S(2)}) copy-start(f32[1,128,512]{2,1,0:T(8,128)} %param.11) | copy-start | bytes 786436
  79.6 5.3 %copy-start.4 = (f32[1,128,512]{2,1,0:T(8,128)S(1)}, f32[1,128,512]{2,1,0:T(8,128)}, u32[]{:S(2)}) copy-start(f32[1,128,512]{2,1,0:T(8,128)} %param.10) | copy-start | bytes 786436
  79.6 7.2 %copy-start.6 = (f32[1,128,512]{2,1,0:T(8,128)S(1)}, f32[1,128,512]{2,1,0:T(8,128)}, u32[]{:S(2)}) copy-start(f32[1,128,512]{2,1,0:T(8,128)} %param.9) | copy-start | bytes 786436
  79.6 7.2 %copy-start.8 = (f32[128,512]{1,0:T(8,128)S(1)}, f32[128,512]{1,0:T(8,128)}, u32[]{:S(2)}) copy-start(f32[128,512]{1,0:T(8,128)} %param.12) | copy-start | bytes 786436
  79.6 7.2 %copy-start.9 = (f32[128,512]{1,0:T(8,128)S(1)}, f32[128,512]{1,0:T(8,128)}, u32[]{:S(2)}) copy-start(f32[128,512]{1,0:T(8,128)} %param.13) | copy-start | bytes 786436
  79.6 7.2 %collective-permute-start.12 = (bf16[128,512]{1,0:T(8,128)(2,1)S(1)}, bf16[128,512]{1,0:T(8,128)(2,1)S(1)}, u32[]{:S(2)}, u32[]{:S(2)}) collective-permute-start(bf16[128,512]{1,0:T(8,128)(2,1)S(1)} %get-tuple-element.23), channel_id=1, source_target_pairs={{0,256},{256,0},{1,257},{257,1},{2,258},{258,2},{3,259},{259,3},{4... | collective-permute-start | bytes 393224 | tf_op jit(solution)/shard_map/ppermute | solution.py:25

commit v5 on v4

--- a/solution.py
+++ b/solution.py
@@ -139,6 +139,7 @@
     four = (wide[0] + wide[1]) + (wide[2] + wide[3])
     come, four = lax.optimization_barrier((come, four))
     part = total(come).astype(BF16)
+    four, part = lax.optimization_barrier((four, part))
     eight = add_other(four, "y", 4)
     summed = add_other(eight, "zl", 1)
 

time: 88.6 us -> 88.6 us (level)
  no operation moved by 1% of the time
where the time goes in v5:
time: 88.6 us; the launch traced here: 87.9 us
  starting transfers between devices  63.1 us (71%)
  other arithmetic  7.94 us (9%)
  waiting for transfers between devices  6.86 us (8%)
  Pallas kernels  6.41 us (7%)
  local copies, waits for them, and re-layouts  2.59 us (3%)
  between operations  0.95 us (1%)
    ppermute x13, starting transfers between devices, trade(): lax.ppermute(block, axis, [(i, i ^ mask) for i in range(lax.axis_size(axi...  53.1 us
    all_to_all x2, starting transfers between devices, exchange(): return lax.all_to_all(blocks, axis, 0, 0, tiled=True)  10.1 us
    ppermute x13, waiting for transfers between devices, trade(): lax.ppermute(block, axis, [(i, i ^ mask) for i in range(lax.axis_size(axi...  6.85 us
    pallas_call x4, Pallas kernels, call(): pl.pallas_call(body, in_specs=[SMEM] + [VMEM] * (count - 1) + [pl.BlockSp...  6.41 us
    reduce_sum x2, other arithmetic, total(): return jnp.sum(blocks.astype(F32), axis=0)  4 us
    unnamed x20, local copies, waits for them, and re-layouts  2.59 us
  transfers between devices with their start and end apart: 15, of which 5 were waited for; matrix products, arithmetic and copies ran while one was open for 8% of the time, Pallas kernels for 3%

profile of v5, /device:TPU:1, one launch (start us, length us, event | category | flops | bytes accessed | tf_op | source)
XLA Modules:
  0.0 87.9 jit_solution(13475722789722805496)
XLA Ops:
  0.6 0.1 pad_add_fusion.refs_0_
  0.7 0.0 copy-start
  0.7 1.6 %copy-done = bf16[256,4096]{1,0:T(8,128)(2,1)S(1)} copy-done((bf16[256,4096]{1,0:T(8,128)(2,1)S(1)}, bf16[256,4096]{1,0:T(8,128)(2,1)}, u32[]{:S(2)}) %copy-start) | copy-done | bytes 2097176
  2.3 0.0 copy-start.2
  2.3 0.9 %copy-done.2 = bf16[256,512]{1,0:T(8,128)(2,1)S(1)} copy-done((bf16[256,512]{1,0:T(8,128)(2,1)S(1)}, bf16[256,512]{1,0:T(8,128)(2,1)}, u32[]{:S(2)}) %copy-start.2) | copy-done | bytes 262168
  3.3 0.8 send.1
  4.0 8.8 %collective-permute-start = (bf16[256,2560]{1,0:T(8,128)(2,1)S(1)}, bf16[256,2560]{1,0:T(8,128)(2,1)S(1)}, u32[]{:S(2)}, u32[]{:S(2)}) collective-permute-start(bf16[256,2560]{1,0:T(8,128)(2,1)S(1)} %send.1), channel_id=1, source_target_pairs={{0,1},{1,0},{2,3},{3,2},{4,5},{5,4},{6,7},{7,6},{8,9},{9,8},{10,11... | collective-permute-start | bytes 3932168 | tf_op jit(solution)/shard_map/ppermute | solution.py:25
  12.8 2.6 %collective-permute-done.refs_3_.refs_1_ = bf16[256,2560]{1,0:T(8,128)(2,1)S(1)} collective-permute-done((bf16[256,2560]{1,0:T(8,128)(2,1)S(1)}, bf16[256,2560]{1,0:T(8,128)(2,1)S(1)}, u32[]{:S(2)}, u32[]{:S(2)}) %collective-permute-start) | collective-permute-done | bytes 1310752 | tf_op jit(solution)/shard_map/ppermute | solution.py:25
  15.5 3.1 %grad.1 = bf16[4,512,512]{2,1,0:T(8,128)(2,1)} custom-call(s32[3]{0:T(128)S(1)} %pad_add_fusion.refs_0_, bf16[256,4096]{1,0:T(8,128)(2,1)S(1)} %copy-done, bf16[256,512]{1,0:T(8,128)(2,1)S(1)} %copy-done.2, bf16[256,2560]{1,0:T(8,128)(2,1)S(1)} %collective-permute-done.refs_3_.refs_1_), custom_call_target="tpu_custom_call" | custom-call | flops 1073741824 | bytes 7340056 | tf_op jit(solution)/shard_map/grad/pallas_call | solution.py:48
  18.6 0.0 copy-start.5
  18.6 4.6 %all-to-all-start = ((bf16[4,512,512]{2,1,0:T(8,128)(2,1)}), bf16[4,512,512]{2,1,0:T(8,128)(2,1)}, u32[]{:S(2)}, u32[]{:S(2)}) async-start(bf16[4,512,512]{2,1,0:T(8,128)(2,1)} %grad.1), calls=%async_computation | async-start | bytes 4194304 | tf_op jit(solution)/shard_map/all_to_all | solution.py:34
  23.2 0.0 copy-done.5
  23.2 1.9 %collective-permute-start.1 = (bf16[128,512]{1,0:T(8,128)(2,1)S(1)}, bf16[128,512]{1,0:T(8,128)(2,1)S(1)}, u32[]{:S(2)}, u32[]{:S(2)}) collective-permute-start(bf16[128,512]{1,0:T(8,128)(2,1)S(1)} %bitcast_convert_fusion), channel_id=1, source_target_pairs={{0,2},{2,0},{4,6},{6,4},{1,3},{3,1},{5,7},{7,5},{8,10},{10,8},{12,... | collective-permute-start | bytes 393224 | tf_op jit(solution)/shard_map/ppermute | solution.py:25
  25.2 5.5 %collective-permute-start.3 = (bf16[128,512]{1,0:T(8,128)(2,1)S(1)}, bf16[128,512]{1,0:T(8,128)(2,1)S(1)}, u32[]{:S(2)}, u32[]{:S(2)}) collective-permute-start(bf16[128,512]{1,0:T(8,128)(2,1)S(1)} %bitcast_convert_fusion), channel_id=1, source_target_pairs={{0,6},{2,4},{4,2},{6,0},{1,7},{3,5},{5,3},{7,1},{8,14},{10,12},{12... | collective-permute-start | bytes 393224 | tf_op jit(solution)/shard_map/ppermute | solution.py:25
  30.7 3.9 %collective-permute-start.2 = (bf16[128,512]{1,0:T(8,128)(2,1)S(1)}, bf16[128,512]{1,0:T(8,128)(2,1)S(1)}, u32[]{:S(2)}, u32[]{:S(2)}) collective-permute-start(bf16[128,512]{1,0:T(8,128)(2,1)S(1)} %bitcast_convert_fusion), channel_id=1, source_target_pairs={{0,4},{2,6},{4,0},{6,2},{1,5},{3,7},{5,1},{7,3},{8,12},{10,14},{12... | collective-permute-start | bytes 393224 | tf_op jit(solution)/shard_map/ppermute | solution.py:25
  34.6 0.0 collective-permute-done.1
  34.7 3.0 %collective-permute-start.4 = (bf16[128,512]{1,0:T(8,128)(2,1)S(1)}, bf16[128,512]{1,0:T(8,128)(2,1)S(1)}, u32[]{:S(2)}, u32[]{:S(2)}) collective-permute-start(bf16[128,512]{1,0:T(8,128)(2,1)S(1)} %bitcast_convert_fusion), channel_id=1, source_target_pairs={{0,32},{32,0},{64,96},{96,64},{128,160},{160,128},{192,224},{224,1... | collective-permute-start | bytes 393224 | tf_op jit(solution)/shard_map/ppermute | solution.py:25
  37.7 4.1 %collective-permute-start.9 = (bf16[128,512]{1,0:T(8,128)(2,1)S(1)}, bf16[128,512]{1,0:T(8,128)(2,1)S(1)}, u32[]{:S(2)}, u32[]{:S(2)}) collective-permute-start(bf16[128,512]{1,0:T(8,128)(2,1)S(1)} %bitcast_convert_fusion), channel_id=1, source_target_pairs={{0,96},{32,64},{64,32},{96,0},{128,224},{160,192},{192,160},{224,1... | collective-permute-start | bytes 393224 | tf_op jit(solution)/shard_map/ppermute | solution.py:25
  41.8 2.0 %collective-permute-start.8 = (bf16[128,512]{1,0:T(8,128)(2,1)S(1)}, bf16[128,512]{1,0:T(8,128)(2,1)S(1)}, u32[]{:S(2)}, u32[]{:S(2)}) collective-permute-start(bf16[128,512]{1,0:T(8,128)(2,1)S(1)} %bitcast_convert_fusion), channel_id=1, source_target_pairs={{0,64},{32,96},{64,0},{96,32},{128,192},{160,224},{192,128},{224,1... | collective-permute-start | bytes 393224 | tf_op jit(solution)/shard_map/ppermute | solution.py:25
  43.8 0.0 collective-permute-done.3
  43.8 0.0 collective-permute-done.2
  43.9 0.0 collective-permute-done.4
  43.9 4.5 %collective-permute-start.7 = (bf16[512,512]{1,0:T(8,128)(2,1)S(1)}, bf16[512,512]{1,0:T(8,128)(2,1)S(1)}, u32[]{:S(2)}, u32[]{:S(2)}) collective-permute-start(bf16[512,512]{1,0:T(8,128)(2,1)S(1)} %pad_maximum_fusion.refs_2_), channel_id=1, source_target_pairs={{0,24},{8,16},{16,8},{24,0},{1,25},{9,17},{17,9},{25,1},{2,26},{10... | collective-permute-start | bytes 1572872 | tf_op jit(solution)/shard_map/ppermute | solution.py:25
  48.4 2.5 %collective-permute-start.6 = (bf16[512,512]{1,0:T(8,128)(2,1)S(1)}, bf16[512,512]{1,0:T(8,128)(2,1)S(1)}, u32[]{:S(2)}, u32[]{:S(2)}) collective-permute-start(bf16[512,512]{1,0:T(8,128)(2,1)S(1)} %pad_maximum_fusion.refs_2_), channel_id=1, source_target_pairs={{0,16},{8,24},{16,0},{24,8},{1,17},{9,25},{17,1},{25,9},{2,18},{10... | collective-permute-start | bytes 1572872 | tf_op jit(solution)/shard_map/ppermute | solution.py:25
  50.9 2.0 %collective-permute-start.5 = (bf16[512,512]{1,0:T(8,128)(2,1)S(1)}, bf16[512,512]{1,0:T(8,128)(2,1)S(1)}, u32[]{:S(2)}, u32[]{:S(2)}) collective-permute-start(bf16[512,512]{1,0:T(8,128)(2,1)S(1)} %pad_maximum_fusion.refs_2_), channel_id=1, source_target_pairs={{0,8},{8,0},{16,24},{24,16},{1,9},{9,1},{17,25},{25,17},{2,10},{10... | collective-permute-start | bytes 1572872 | tf_op jit(solution)/shard_map/ppermute | solution.py:25
  52.9 0.0 collective-permute-done.9
  52.9 0.4 collective-permute-done.8
  53.3 0.1 add_add_fusion
  53.3 0.0 copy-start.7
  53.4 0.0 all-to-all-done
  53.4 2.9 %reduce_sum.21.refs_6_ = bf16[512,512]{1,0:T(8,128)(2,1)} reduce(bf16[4,512,512]{2,1,0:T(8,128)(2,1)} %all-to-all-done, bf16[]{:T(256)} %constant.9.clone.1), dimensions={0}, to_apply=%region_0.0 | reduce | flops 786432 | bytes 2621442 | tf_op jit(solution)/shard_map/reduce_sum | solution.py:38
  56.2 7.0 %collective-permute-start.10 = (bf16[128,512]{1,0:T(8,128)(2,1)S(1)}, bf16[128,512]{1,0:T(8,128)(2,1)}, u32[]{:S(2)}, u32[]{:S(2)}) collective-permute-start(bf16[128,512]{1,0:T(8,128)(2,1)S(1)} %add_add_fusion), channel_id=1, source_target_pairs={{0,128},{32,160},{64,192},{96,224},{128,0},{160,32},{192,64},{224,... | collective-permute-start | bytes 393224 | tf_op jit(solution)/shard_map/ppermute | solution.py:25
  63.2 5.5 %all-to-all-start.1 = ((bf16[4,128,512]{2,1,0:T(8,128)(2,1)}), bf16[4,128,512]{2,1,0:T(8,128)(2,1)}, u32[]{:S(2)}, u32[]{:S(2)}) async-start(bf16[4,128,512]{2,1,0:T(8,128)(2,1)} %bitcast.5), calls=%async_computation.1 | async-start | bytes 1048576 | tf_op jit(solution)/shard_map/all_to_all | solution.py:34
  68.7 0.0 copy-done.7
  68.7 0.0 collective-permute-done.10
  68.7 1.0 %fusion.7 = (bf16[128,512]{1,0:T(8,128)(2,1)S(1)}, f32[128,512]{1,0:T(8,128)S(1)}) fusion(bf16[128,512]{1,0:T(8,128)(2,1)} %collective-permute-done.10, bf16[128,512]{1,0:T(8,128)(2,1)} %copy-done.7), kind=kLoop, calls=%fused_computation.24 | loop fusion | flops 262144 | bytes 655360 | tf_op jit(solution)/shard_map/convert_element_type | solution.py:29
  69.7 1.1 %collective-permute-done.7.refs_5_ = bf16[512,512]{1,0:T(8,128)(2,1)S(1)} collective-permute-done((bf16[512,512]{1,0:T(8,128)(2,1)S(1)}, bf16[512,512]{1,0:T(8,128)(2,1)S(1)}, u32[]{:S(2)}, u32[]{:S(2)}) %collective-permute-start.7) | collective-permute-done | bytes 524320 | tf_op jit(solution)/shard_map/ppermute | solution.py:25
  70.8 0.0 collective-permute-done.6.refs_4_
  70.8 1.7 %collective-permute-done.5.refs_3_ = bf16[512,512]{1,0:T(8,128)(2,1)S(1)} collective-permute-done((bf16[512,512]{1,0:T(8,128)(2,1)S(1)}, bf16[512,512]{1,0:T(8,128)(2,1)S(1)}, u32[]{:S(2)}, u32[]{:S(2)}) %collective-permute-start.5) | collective-permute-done | bytes 524320 | tf_op jit(solution)/shard_map/ppermute | solution.py:25
  72.5 0.0 copy-start.1
  72.5 1.2 %their_keys.1 = f32[256,512]{1,0:T(8,128)S(1)} custom-call(s32[3]{0:T(128)S(1)} %pad_add_fusion.refs_0_, bf16[256,2560]{1,0:T(8,128)(2,1)S(1)} %collective-permute-done.refs_3_.refs_1_, bf16[512,512]{1,0:T(8,128)(2,1)S(1)} %pad_maximum_fusion.refs_2_, bf16[512,512]{1,0:T(8,128)(2,1)S(1)} %collective-permute-done.5.refs_3_, ...), custom_call_target="tpu_custom_call" | custom-call | flops 536870912 | bytes 6815768 | tf_op jit(solution)/shard_map/their_keys/pallas_call | solution.py:48
  73.7 4.6 %collective-permute-start.11 = (f32[256,512]{1,0:T(8,128)S(1)}, f32[256,512]{1,0:T(8,128)S(1)}, u32[]{:S(2)}, u32[]{:S(2)}) collective-permute-start(f32[256,512]{1,0:T(8,128)S(1)} %their_keys.1), channel_id=1, source_target_pairs={{0,1},{1,0},{2,3},{3,2},{4,5},{5,4},{6,7},{7,6},{8,9},{9,8},{10,11... | collective-permute-start | bytes 1572872 | tf_op jit(solution)/shard_map/ppermute | solution.py:25
  78.3 0.0 copy-done.1
  78.3 1.3 %our_keys.1 = f32[256,512]{1,0:T(8,128)S(1)} custom-call(s32[3]{0:T(128)S(1)} %pad_add_fusion.refs_0_, bf16[256,4096]{1,0:T(8,128)(2,1)S(1)} %copy-done.1, bf16[512,512]{1,0:T(8,128)(2,1)S(1)} %pad_maximum_fusion.refs_2_, bf16[512,512]{1,0:T(8,128)(2,1)S(1)} %collective-permute-done.5.refs_3_, bf16[512,512]{1,0:T(8,128)(2,1)S(1)} %collective-permute-done.6.refs_4_, ...), custom_call_target="tpu_custom_call" | custom-call | flops 536870912 | bytes 8388632 | tf_op jit(solution)/shard_map/our_keys/pallas_call | solution.py:48
  79.6 0.0 copy-start.3
  79.6 0.0 copy-start.4
  79.6 0.0 copy-start.6
  79.6 0.0 copy-start.8
  79.6 0.0 copy-start.9
  79.6 3.2 %collective-permute-start.12 = (bf16[128,512]{1,0:T(8,128)(2,1)S(1)}, bf16[128,512]{1,0:T(8,128)(2,1)S(1)}, u32[]{:S(2)}, u32[]{:S(2)}) collective-permute-start(bf16[128,512]{1,0:T(8,128)(2,1)S(1)} %get-tuple-element.27), channel_id=1, source_target_pairs={{0,256},{256,0},{1,257},{257,1},{2,258},{258,2},{3,259},{259,3},{4... | collective-permute-start | bytes 393224 | tf_op jit(solution)/shard_map/ppermute | solution.py:25
  82.9 0.0 collective-permute-done.11
  82.9 0.8 multiply_convert_fusion
  83.7 0.0 all-to-all-done.1
  83.7 1.1 %convert_reduce_fusion = f32[128,512]{1,0:T(8,128)S(1)} fusion(bf16[4,128,512]{2,1,0:T(8,128)(2,1)} %all-to-all-done.1), kind=kLoop, calls=%fused_computation | loop fusion | flops 458752 | bytes 786432 | tf_op jit(solution)/shard_map/reduce_sum | solution.py:38
  84.9 0.0 copy-done.3
  84.9 0.0 copy-done.4
  84.9 0.9 %bitcast_add_fusion = (f32[1,128,512]{2,1,0:T(8,128)}, f32[1,128,512]{2,1,0:T(8,128)}) fusion(f32[1,128,512]{2,1,0:T(8,128)S(1)} %copy-done.3, f32[128,512]{1,0:T(8,128)S(1)} %convert_reduce_fusion, f32[1,128,512]{2,1,0:T(8,128)S(1)} %copy-done.4), kind=kLoop, calls=%fused_computation.3 | loop fusion | flops 524288 | bytes 1310720 | tf_op jit(solution)/shard_map/add | solution.py:164
  85.8 1.1 %collective-permute-done.12 = bf16[128,512]{1,0:T(8,128)(2,1)S(1)} collective-permute-done((bf16[128,512]{1,0:T(8,128)(2,1)S(1)}, bf16[128,512]{1,0:T(8,128)(2,1)S(1)}, u32[]{:S(2)}, u32[]{:S(2)}) %collective-permute-start.12) | collective-permute-done | bytes 131104 | tf_op jit(solution)/shard_map/ppermute | solution.py:25
  86.8 0.0 copy-done.6
  86.8 0.0 copy-done.8
  86.8 0.0 copy-done.9
  86.8 1.0 %multiply_bitcast_fusion = (f32[1,128,512]{2,1,0:T(8,128)}, f32[128,512]{1,0:T(8,128)}, f32[128,512]{1,0:T(8,128)}) fusion(f32[1,128,512]{2,1,0:T(8,128)S(1)} %copy-done.6, f32[1,128,512]{2,1,0:T(8,128)S(1)} %copy-done.3, f32[128,512]{1,0:T(8,128)S(1)} %convert_reduce_fusion, f32[1,128,512]{2,1,0:T(8,128)S(1)} %copy-done.4, f32[128,512]{1,0:T(8,128)S(1)} %copy-done.8, ...), kind=kLoop, calls=%fused_computation.16 | loop fusion | flops 1769472 | bytes 2621440 | tf_op jit(solution)/shard_map/broadcast_in_dim | solution.py:168
  (2 shorter events, 0.1 us)
Async XLA Ops:
  0.7 1.6 %copy-start = (bf16[256,4096]{1,0:T(8,128)(2,1)S(1)}, bf16[256,4096]{1,0:T(8,128)(2,1)}, u32[]{:S(2)}) copy-start(bf16[256,4096]{1,0:T(8,128)(2,1)} %refs_1_.5) | copy-start | bytes 6291460
  2.3 0.9 %copy-start.2 = (bf16[256,512]{1,0:T(8,128)(2,1)S(1)}, bf16[256,512]{1,0:T(8,128)(2,1)}, u32[]{:S(2)}) copy-start(bf16[256,512]{1,0:T(8,128)(2,1)} %refs_2_.3) | copy-start | bytes 786436
  4.0 11.4 %collective-permute-start = (bf16[256,2560]{1,0:T(8,128)(2,1)S(1)}, bf16[256,2560]{1,0:T(8,128)(2,1)S(1)}, u32[]{:S(2)}, u32[]{:S(2)}) collective-permute-start(bf16[256,2560]{1,0:T(8,128)(2,1)S(1)} %send.1), channel_id=1, source_target_pairs={{0,1},{1,0},{2,3},{3,2},{4,5},{5,4},{6,7},{7,6},{8,9},{9,8},{10,11... | collective-permute-start | bytes 3932168 | tf_op jit(solution)/shard_map/ppermute | solution.py:25
  18.6 4.6 %copy-start.5 = (f32[1,128,512]{2,1,0:T(8,128)S(1)}, f32[1,128,512]{2,1,0:T(8,128)}, u32[]{:S(2)}) copy-start(f32[1,128,512]{2,1,0:T(8,128)} %param.9) | copy-start | bytes 786436
  18.6 34.8 %all-to-all-start = ((bf16[4,512,512]{2,1,0:T(8,128)(2,1)}), bf16[4,512,512]{2,1,0:T(8,128)(2,1)}, u32[]{:S(2)}, u32[]{:S(2)}) async-start(bf16[4,512,512]{2,1,0:T(8,128)(2,1)} %grad.1), calls=%async_computation | async-start | bytes 4194304 | tf_op jit(solution)/shard_map/all_to_all | solution.py:34
  23.2 11.4 %collective-permute-start.1 = (bf16[128,512]{1,0:T(8,128)(2,1)S(1)}, bf16[128,512]{1,0:T(8,128)(2,1)S(1)}, u32[]{:S(2)}, u32[]{:S(2)}) collective-permute-start(bf16[128,512]{1,0:T(8,128)(2,1)S(1)} %bitcast_convert_fusion), channel_id=1, source_target_pairs={{0,2},{2,0},{4,6},{6,4},{1,3},{3,1},{5,7},{7,5},{8,10},{10,8},{12,... | collective-permute-start | bytes 393224 | tf_op jit(solution)/shard_map/ppermute | solution.py:25
  25.2 18.7 %collective-permute-start.3 = (bf16[128,512]{1,0:T(8,128)(2,1)S(1)}, bf16[128,512]{1,0:T(8,128)(2,1)S(1)}, u32[]{:S(2)}, u32[]{:S(2)}) collective-permute-start(bf16[128,512]{1,0:T(8,128)(2,1)S(1)} %bitcast_convert_fusion), channel_id=1, source_target_pairs={{0,6},{2,4},{4,2},{6,0},{1,7},{3,5},{5,3},{7,1},{8,14},{10,12},{12... | collective-permute-start | bytes 393224 | tf_op jit(solution)/shard_map/ppermute | solution.py:25
  30.7 13.1 %collective-permute-start.2 = (bf16[128,512]{1,0:T(8,128)(2,1)S(1)}, bf16[128,512]{1,0:T(8,128)(2,1)S(1)}, u32[]{:S(2)}, u32[]{:S(2)}) collective-permute-start(bf16[128,512]{1,0:T(8,128)(2,1)S(1)} %bitcast_convert_fusion), channel_id=1, source_target_pairs={{0,4},{2,6},{4,0},{6,2},{1,5},{3,7},{5,1},{7,3},{8,12},{10,14},{12... | collective-permute-start | bytes 393224 | tf_op jit(solution)/shard_map/ppermute | solution.py:25
  34.7 9.2 %collective-permute-start.4 = (bf16[128,512]{1,0:T(8,128)(2,1)S(1)}, bf16[128,512]{1,0:T(8,128)(2,1)S(1)}, u32[]{:S(2)}, u32[]{:S(2)}) collective-permute-start(bf16[128,512]{1,0:T(8,128)(2,1)S(1)} %bitcast_convert_fusion), channel_id=1, source_target_pairs={{0,32},{32,0},{64,96},{96,64},{128,160},{160,128},{192,224},{224,1... | collective-permute-start | bytes 393224 | tf_op jit(solution)/shard_map/ppermute | solution.py:25
  37.7 15.2 %collective-permute-start.9 = (bf16[128,512]{1,0:T(8,128)(2,1)S(1)}, bf16[128,512]{1,0:T(8,128)(2,1)S(1)}, u32[]{:S(2)}, u32[]{:S(2)}) collective-permute-start(bf16[128,512]{1,0:T(8,128)(2,1)S(1)} %bitcast_convert_fusion), channel_id=1, source_target_pairs={{0,96},{32,64},{64,32},{96,0},{128,224},{160,192},{192,160},{224,1... | collective-permute-start | bytes 393224 | tf_op jit(solution)/shard_map/ppermute | solution.py:25
  41.8 11.5 %collective-permute-start.8 = (bf16[128,512]{1,0:T(8,128)(2,1)S(1)}, bf16[128,512]{1,0:T(8,128)(2,1)S(1)}, u32[]{:S(2)}, u32[]{:S(2)}) collective-permute-start(bf16[128,512]{1,0:T(8,128)(2,1)S(1)} %bitcast_convert_fusion), channel_id=1, source_target_pairs={{0,64},{32,96},{64,0},{96,32},{128,192},{160,224},{192,128},{224,1... | collective-permute-start | bytes 393224 | tf_op jit(solution)/shard_map/ppermute | solution.py:25
  43.9 26.9 %collective-permute-start.7 = (bf16[512,512]{1,0:T(8,128)(2,1)S(1)}, bf16[512,512]{1,0:T(8,128)(2,1)S(1)}, u32[]{:S(2)}, u32[]{:S(2)}) collective-permute-start(bf16[512,512]{1,0:T(8,128)(2,1)S(1)} %pad_maximum_fusion.refs_2_), channel_id=1, source_target_pairs={{0,24},{8,16},{16,8},{24,0},{1,25},{9,17},{17,9},{25,1},{2,26},{10... | collective-permute-start | bytes 1572872 | tf_op jit(solution)/shard_map/ppermute | solution.py:25
  48.4 22.4 %collective-permute-start.6 = (bf16[512,512]{1,0:T(8,128)(2,1)S(1)}, bf16[512,512]{1,0:T(8,128)(2,1)S(1)}, u32[]{:S(2)}, u32[]{:S(2)}) collective-permute-start(bf16[512,512]{1,0:T(8,128)(2,1)S(1)} %pad_maximum_fusion.refs_2_), channel_id=1, source_target_pairs={{0,16},{8,24},{16,0},{24,8},{1,17},{9,25},{17,1},{25,9},{2,18},{10... | collective-permute-start | bytes 1572872 | tf_op jit(solution)/shard_map/ppermute | solution.py:25
  50.9 21.5 %collective-permute-start.5 = (bf16[512,512]{1,0:T(8,128)(2,1)S(1)}, bf16[512,512]{1,0:T(8,128)(2,1)S(1)}, u32[]{:S(2)}, u32[]{:S(2)}) collective-permute-start(bf16[512,512]{1,0:T(8,128)(2,1)S(1)} %pad_maximum_fusion.refs_2_), channel_id=1, source_target_pairs={{0,8},{8,0},{16,24},{24,16},{1,9},{9,1},{17,25},{25,17},{2,10},{10... | collective-permute-start | bytes 1572872 | tf_op jit(solution)/shard_map/ppermute | solution.py:25
  53.3 15.3 %copy-start.7 = (bf16[128,512]{1,0:T(8,128)(2,1)}, bf16[128,512]{1,0:T(8,128)(2,1)S(1)}, u32[]{:S(2)}) copy-start(bf16[128,512]{1,0:T(8,128)(2,1)S(1)} %add_add_fusion) | copy-start | bytes 393220
  56.2 12.4 %collective-permute-start.10 = (bf16[128,512]{1,0:T(8,128)(2,1)S(1)}, bf16[128,512]{1,0:T(8,128)(2,1)}, u32[]{:S(2)}, u32[]{:S(2)}) collective-permute-start(bf16[128,512]{1,0:T(8,128)(2,1)S(1)} %add_add_fusion), channel_id=1, source_target_pairs={{0,128},{32,160},{64,192},{96,224},{128,0},{160,32},{192,64},{224,... | collective-permute-start | bytes 393224 | tf_op jit(solution)/shard_map/ppermute | solution.py:25
  63.2 20.5 %all-to-all-start.1 = ((bf16[4,128,512]{2,1,0:T(8,128)(2,1)}), bf16[4,128,512]{2,1,0:T(8,128)(2,1)}, u32[]{:S(2)}, u32[]{:S(2)}) async-start(bf16[4,128,512]{2,1,0:T(8,128)(2,1)} %bitcast.5), calls=%async_computation.1 | async-start | bytes 1048576 | tf_op jit(solution)/shard_map/all_to_all | solution.py:34
  72.5 5.8 %copy-start.1 = (bf16[256,4096]{1,0:T(8,128)(2,1)S(1)}, bf16[256,4096]{1,0:T(8,128)(2,1)}, u32[]{:S(2)}) copy-start(bf16[256,4096]{1,0:T(8,128)(2,1)} %refs_1_.5) | copy-start | bytes 6291460
  73.7 9.2 %collective-permute-start.11 = (f32[256,512]{1,0:T(8,128)S(1)}, f32[256,512]{1,0:T(8,128)S(1)}, u32[]{:S(2)}, u32[]{:S(2)}) collective-permute-start(f32[256,512]{1,0:T(8,128)S(1)} %their_keys.1), channel_id=1, source_target_pairs={{0,1},{1,0},{2,3},{3,2},{4,5},{5,4},{6,7},{7,6},{8,9},{9,8},{10,11... | collective-permute-start | bytes 1572872 | tf_op jit(solution)/shard_map/ppermute | solution.py:25
  79.6 5.3 %copy-start.3 = (f32[1,128,512]{2,1,0:T(8,128)S(1)}, f32[1,128,512]{2,1,0:T(8,128)}, u32[]{:S(2)}) copy-start(f32[1,128,512]{2,1,0:T(8,128)} %param.11) | copy-start | bytes 786436
  79.6 5.3 %copy-start.4 = (f32[1,128,512]{2,1,0:T(8,128)S(1)}, f32[1,128,512]{2,1,0:T(8,128)}, u32[]{:S(2)}) copy-start(f32[1,128,512]{2,1,0:T(8,128)} %param.10) | copy-start | bytes 786436
  79.6 7.2 %copy-start.6 = (f32[1,128,512]{2,1,0:T(8,128)S(1)}, f32[1,128,512]{2,1,0:T(8,128)}, u32[]{:S(2)}) copy-start(f32[1,128,512]{2,1,0:T(8,128)} %param.9) | copy-start | bytes 786436
  79.6 7.2 %copy-start.8 = (f32[128,512]{1,0:T(8,128)S(1)}, f32[128,512]{1,0:T(8,128)}, u32[]{:S(2)}) copy-start(f32[128,512]{1,0:T(8,128)} %param.12) | copy-start | bytes 786436
  79.6 7.2 %copy-start.9 = (f32[128,512]{1,0:T(8,128)S(1)}, f32[128,512]{1,0:T(8,128)}, u32[]{:S(2)}) copy-start(f32[128,512]{1,0:T(8,128)} %param.13) | copy-start | bytes 786436
  79.6 7.2 %collective-permute-start.12 = (bf16[128,512]{1,0:T(8,128)(2,1)S(1)}, bf16[128,512]{1,0:T(8,128)(2,1)S(1)}, u32[]{:S(2)}, u32[]{:S(2)}) collective-permute-start(bf16[128,512]{1,0:T(8,128)(2,1)S(1)} %get-tuple-element.27), channel_id=1, source_target_pairs={{0,256},{256,0},{1,257},{257,1},{2,258},{258,2},{3,259},{259,3},{4... | collective-permute-start | bytes 393224 | tf_op jit(solution)/shard_map/ppermute | solution.py:25
